TPU v7x, 512 devices: a whole 4x4x16 slice. The times are simulated.
512 devices in a mesh: tiles: 128 (over z, x, core), far: 4 (over y).
Axes of the slice: x: 4, y: 4, z: 16, core: 2. Of those that a mesh axis runs over, the one named last changes fastest.
Arguments:
- panel_geometry: float32 [512, 6, 128], P('tiles'), may hold values from -1 to 1
- adjoint: bfloat16 [512, 16, 128], P('tiles', 'far'), may hold values from -6 to 6
- strengths: bfloat16 [512, 16, 128], P('tiles', 'far'), may hold values from -6 to 6
- pair_target: int32 [4096], P('tiles'), may hold values from 0 to 3
- pair_owner: int32 [4096, 1], P('tiles'), may hold values from 0 to 127; in each aligned block of 32 rows (0 to 31, 32 to 63, ...) at most 2 rows name the same one
- pair_source: int32 [4096], P('tiles'), may hold values from 0 to 3
- pair_order: int32 [4096], P('tiles'), may hold values from 1 to 3
- pair_count: int32 [128], P('tiles'), may hold values from 24 to 32, as said below
- corner_vertex: int32 [512, 4, 128], P('tiles'), may hold values from 0 to 65535, as said below
Outputs:
- vertex_grad: float32 [3, 65536], P(None, 'tiles')
Inputs may be any that keep to these rules, and one draw needn't show every extreme that they name: `pair_owner`: in the 32 slots of one list no owner is named more than 2 times; some list names one owner exactly 2 times. `pair_count`: some list is full with 32 live pairs. `corner_vertex`: every corner of a panel on tiles index t is a vertex owned by index t, t - 1, t + 1 or t + 128 / 2 (cyclically; the last is the mirrored half of the airframe); vertex v is owned by index v // 512.
All inputs are finite; a program needn't handle non-finite values.
Results may differ from a plain program's by a relative error of at most 0.00035.
Values may be sent and summed in bfloat16 or wider, within the bound.
A program may use at most 128 MiB of HBM per device.

v0:
```python
import jax
import jax.numpy as jnp
from jax import lax
from jax.sharding import PartitionSpec as P

PAIRS_DEV = 32


def quadrature(orders):
    first = (orders == 1)[:, None]
    second = (orders == 2)[:, None]
    root_half = 0.5773502691896258
    root_fifth = 0.7745966692414834
    nodes = jnp.where(
        first,
        jnp.array([0.0, 0.0, 0.0], dtype=jnp.float32),
        jnp.where(
            second,
            jnp.array([-root_half, root_half, 0.0], dtype=jnp.float32),
            jnp.array([0.0, -root_fifth, root_fifth], dtype=jnp.float32),
        ),
    )
    weights = jnp.where(
        first,
        jnp.array([1.0, 0.0, 0.0], dtype=jnp.float32),
        jnp.where(
            second,
            jnp.array([0.5, 0.5, 0.0], dtype=jnp.float32),
            jnp.array([4.0 / 9.0, 5.0 / 18.0, 5.0 / 18.0], dtype=jnp.float32),
        ),
    )
    return (nodes, weights)


def tile_terms(target_geom, target_adjoint, source_geom, source_strength, orders):
    panel_coupling = jnp.einsum(
        "avk,avu->aku", target_adjoint, source_strength, preferred_element_type=jnp.float32
    )
    nodes, weights = quadrature(orders)
    centre = target_geom[:, 0:3]
    target_grad = jnp.zeros(centre.shape, jnp.float32)
    source_grad = jnp.zeros(centre.shape, jnp.float32)
    for gauss_node_index in range(3):
        points = (
            source_geom[:, 0:3]
            + 0.25 * nodes[:, gauss_node_index, None, None] * source_geom[:, 3:6]
        )
        squared = jnp.full(panel_coupling.shape, 0.0625, jnp.float32)
        for comp_index in range(3):
            differ = centre[:, comp_index, :, None] - points[:, comp_index, None, :]
            squared = squared + differ * differ
        factor = (
            weights[:, gauss_node_index, None, None]
            * panel_coupling
            / (squared * jnp.sqrt(squared))
        )
        row_total = jnp.sum(factor, axis=2)
        col_total = jnp.sum(factor, axis=1)
        factor_points = jnp.einsum("apq,acq->acp", factor, points, precision=lax.Precision.HIGHEST)
        factor_centre = jnp.einsum("apq,acp->acq", factor, centre, precision=lax.Precision.HIGHEST)
        target_grad = target_grad - (centre * row_total[:, None] - factor_points)
        source_grad = source_grad + (factor_centre - points * col_total[:, None])
    return (target_grad * 0.0078125, source_grad * 0.0078125)


def per_device(
    panel_geometry,
    adjoint,
    strengths,
    pair_target,
    pair_owner,
    pair_source,
    pair_order,
    pair_count,
    corner_vertex,
):
    tile_count = lax.axis_size("tiles")
    block_count = panel_geometry.shape[0]
    panel_width = panel_geometry.shape[2]
    owners = pair_owner[:, 0]
    live_count = pair_count[0]
    adjoint_part, strength_part = (adjoint, strengths)
    targets, source_ids, orders = (pair_target, pair_source, pair_order)
    pair_total = targets.shape[0]
    capacity = max(2, 2 * PAIRS_DEV // tile_count)
    one_hot = (owners[:, None] == jnp.arange(tile_count, dtype=jnp.int32)[None, :]).astype(
        jnp.int32
    )
    earlier = jnp.cumsum(one_hot, axis=0) - one_hot
    slot_ids = jnp.sum(earlier * one_hot, axis=1)
    wanted = jnp.zeros((tile_count, capacity), jnp.int32).at[owners, slot_ids].set(source_ids)
    asked = lax.all_to_all(wanted, "tiles", split_axis=0, concat_axis=0, tiled=True)
    got_shapes = lax.all_to_all(
        panel_geometry[asked], "tiles", split_axis=0, concat_axis=0, tiled=True
    )
    got_values = lax.all_to_all(
        strength_part[asked], "tiles", split_axis=0, concat_axis=0, tiled=True
    )
    source_shapes = got_shapes[owners, slot_ids]
    source_values = got_values[owners, slot_ids]
    group_rows = 8

    def accumulate(group_index, carried):
        target_acc, source_acc = carried
        start_row = group_index * group_rows
        group_targets = lax.dynamic_slice_in_dim(targets, start_row, group_rows, 0)
        group_shapes = lax.dynamic_slice_in_dim(source_shapes, start_row, group_rows, 0)
        group_values = lax.dynamic_slice_in_dim(source_values, start_row, group_rows, 0)
        group_orders = lax.dynamic_slice_in_dim(orders, start_row, group_rows, 0)
        alive = (start_row + jnp.arange(group_rows, dtype=jnp.int32) < live_count).astype(
            jnp.float32
        )[:, None, None]
        target_grad, source_grad = tile_terms(
            panel_geometry[group_targets],
            adjoint_part[group_targets],
            group_shapes,
            group_values,
            group_orders,
        )
        target_acc = target_acc.at[group_targets].add(target_grad * alive)
        source_acc = lax.dynamic_update_slice_in_dim(source_acc, source_grad * alive, start_row, 0)
        return (target_acc, source_acc)

    trips = (live_count + group_rows - 1) // group_rows
    start_acc = (
        jnp.zeros((block_count, 3, panel_width), jnp.float32),
        jnp.zeros((pair_total, 3, panel_width), jnp.float32),
    )
    target_acc, source_acc = lax.fori_loop(0, trips, accumulate, start_acc)
    table = (
        jnp.zeros((tile_count, capacity, 3, panel_width), jnp.float32)
        .at[owners, slot_ids]
        .add(source_acc)
    )
    returned = lax.all_to_all(table, "tiles", split_axis=0, concat_axis=0, tiled=True)
    panel_grad = target_acc.at[asked.reshape(-1)].add(
        returned.reshape(tile_count * capacity, 3, panel_width)
    )
    panel_grad = lax.psum(panel_grad, "far")
    vertex_width = block_count * panel_width
    corner_values = jnp.broadcast_to(
        0.25 * panel_grad[:, :, None, :], (block_count, 3, 4, panel_width)
    )
    corner_values = corner_values.transpose(1, 0, 2, 3).reshape(3, -1)
    flat_ids = corner_vertex.reshape(-1)
    running_partial_sum = (
        jnp.zeros((3, tile_count * vertex_width), jnp.float32).at[:, flat_ids].add(corner_values)
    )
    vertex_grad = lax.psum_scatter(running_partial_sum, "tiles", scatter_dimension=1, tiled=True)
    return vertex_grad


def solution(mesh):
    placed = (
        P("tiles", None, None),
        P("tiles", "far", None),
        P("tiles", "far", None),
        P("tiles"),
        P("tiles", None),
        P("tiles"),
        P("tiles"),
        P("tiles"),
        P("tiles", None, None),
    )
    return jax.shard_map(
        per_device, mesh=mesh, in_specs=placed, out_specs=P(None, "tiles"), check_vma=False
    )
```

profile of v0, /device:TPU:1, one launch (start us, length us, event | category | flops | bytes accessed | tf_op | source)
XLA Modules:
  0.0 682.7 jit_solution(1585807001704535604)
XLA Ops:
  8.8 3.1 scatter_fusion.1
  12.1 35.1 %all_to_all.27 = s32[128,1,2]{2,1,0:T(1,128)S(1)} all-to-all(s32[128,1,2]{2,1,0:T(1,128)S(1)} %copy.48), channel_id=1, replica_groups=mesh['tiles'=128,'far'=4] {'tiles'}, dimensions={0} | all-to-all | bytes 2048 | tf_op jit(solution)/shard_map/all_to_all | solution.py:92
  47.4 1.7 gather_fusion.2
  49.0 5.7 all-to-all-start.1
  54.7 2.7 gather_fusion.4
  58.5 16.8 %all-to-all-done.1 = bf16[128,2,4,128]{3,2,1,0:T(4,128)(2,1)S(1)} async-done(((bf16[128,2,4,128]{3,2,1,0:T(4,128)(2,1)}), bf16[128,2,4,128]{3,2,1,0:T(4,128)(2,1)S(1)}, u32[]{:S(2)}, u32[]{:S(2)}) %all-to-all-start.1) | async-done | bytes 262176 | tf_op jit(solution)/shard_map/all_to_all | solution.py:96
  75.3 8.4 %all-to-all-start.2 = ((f32[128,2,6,128]{3,1,2,0:T(2,128)}), f32[128,2,6,128]{3,1,2,0:T(2,128)S(1)}, u32[]{:S(2)}, u32[]{:S(2)}) async-start(f32[128,2,6,128]{3,1,2,0:T(2,128)} %copy.49), calls=%async_computation.2 | async-start | bytes 1572864 | tf_op jit(solution)/shard_map/all_to_all | solution.py:93
  85.8 39.4 %all-to-all-done.2 = f32[128,2,6,128]{3,1,2,0:T(2,128)S(1)} async-done(((f32[128,2,6,128]{3,1,2,0:T(2,128)}), f32[128,2,6,128]{3,1,2,0:T(2,128)S(1)}, u32[]{:S(2)}, u32[]{:S(2)}) %all-to-all-start.2) | async-done | bytes 786464 | tf_op jit(solution)/shard_map/all_to_all | solution.py:93
  126.0 48.5 %while.13 = (s32[]{:T(128)}, f32[4,3,128]{2,1,0:T(4,128)S(1)}, f32[32,3,128]{2,1,0:T(4,128)S(1)}, s32[]{:T(128)}, s32[32]{0:T(128)}, /*index=5*/f32[4,6,128]{2,1...) while((s32[]{:T(128)}, f32[4,3,128]{2,1,0:T(4,128)S(1)}, ...), condition=%wide.region_11.12_spmd.clone, body=%wide.region_3.11_spmd.sunk.clone.sunk | while | flops 34940096 | bytes 5410099 | solution.py:129
  129.1 1.3 gather_fusion.1
  131.1 1.9 fusion.83
  141.2 1.3 gather_fusion.1
  143.2 1.9 fusion.83
  155.3 1.9 fusion.83
  165.4 1.3 gather_fusion.1
  167.4 1.9 fusion.83
  174.6 2.0 scatter_fusion.2
  177.6 9.5 %all-to-all-start.3 = ((f32[128,2,3,128]{3,1,2,0:T(2,128)}), f32[128,2,3,128]{3,1,2,0:T(2,128)S(1)}, u32[]{:S(2)}, u32[]{:S(2)}) async-start(f32[128,2,3,128]{3,1,2,0:T(2,128)} %copy.52), calls=%async_computation.3 | async-start | bytes 786432 | tf_op jit(solution)/shard_map/all_to_all | solution.py:135
  188.6 23.9 %all-to-all-done.3 = f32[128,2,3,128]{3,1,2,0:T(2,128)S(1)} async-done(((f32[128,2,3,128]{3,1,2,0:T(2,128)}), f32[128,2,3,128]{3,1,2,0:T(2,128)S(1)}, u32[]{:S(2)}, u32[]{:S(2)}) %all-to-all-start.3) | async-done | bytes 393248 | tf_op jit(solution)/shard_map/all_to_all | solution.py:135
  212.9 9.0 %scatter_fusion.3 = f32[4,3,128]{2,1,0:T(4,128)S(1)} fusion(f32[4,3,128]{2,1,0:T(4,128)S(1)} %get-tuple-element.94, s32[256]{0:T(256)S(1)} %bitcast.132, f32[256,3,128]{2,1,0:T(4,128)S(1)} %copy.54), kind=kCustom, calls=%fused_computation.9 | custom fusion | flops 98304 | bytes 1180672 | tf_op jit(solution)/shard_map/scatter-add | solution.py:136
  221.9 9.0 %psum.7 = f32[4,3,128]{2,0,1:T(4,128)S(1)} all-reduce(f32[4,3,128]{2,0,1:T(4,128)S(1)} %copy.55), channel_id=1, replica_groups=mesh['tiles'=128,'far'=4] {'far'}, use_global_device_ids=true, to_apply=%region_14.15 | all-reduce | flops 1536 | bytes 12288 | tf_op jit(solution)/shard_map/psum | solution.py:139
  231.3 24.6 %scatter_custom_fusion.4 = f32[3,65536]{0,1:T(8,128)} fusion(s32[2048]{0:T(1024)S(1)} %bitcast.129, f32[2048,3]{1,0:T(8,128)S(1)} %bitcast.114, f32[]{:T(128)} %constant.80.clone), kind=kCustom, calls=%fused_computation.53 | custom fusion | flops 6144 | bytes 786436 | tf_op jit(solution)/shard_map/scatter-add | solution.py:147
  255.9 418.3 %reduce-scatter.2.cloned.1.call-done = f32[3,512]{0,1:T(8,128)} async-done(((f32[3,65536]{0,1:T(8,128)}), f32[3,512]{0,1:T(8,128)}) %reduce-scatter.2.cloned.1.call-update) | async-done | bytes 6160 | tf_op jit(solution)/shard_map/reduce_scatter | solution.py:149
  674.2 1.7 copy.57
  (112 shorter events, 45.6 us)
Async XLA Ops:
  6.5 40.8 %copy-start = (bf16[4,4,128]{2,1,0:T(4,128)(2,1)S(1)}, bf16[4,4,128]{2,1,0:T(4,128)(2,1)}, u32[]{:S(2)}) copy-start(bf16[4,4,128]{2,1,0:T(4,128)(2,1)} %param.19) | copy-start | bytes 12292
  49.0 26.3 %all-to-all-start.1 = ((bf16[128,2,4,128]{3,2,1,0:T(4,128)(2,1)}), bf16[128,2,4,128]{3,2,1,0:T(4,128)(2,1)S(1)}, u32[]{:S(2)}, u32[]{:S(2)}) async-start(bf16[128,2,4,128]{3,2,1,0:T(4,128)(2,1)} %bitcast.8), calls=%async_computation.1 | async-start | bytes 524288 | tf_op jit(solution)/shard_map/all_to_all | solution.py:96
  75.3 49.8 %all-to-all-start.2 = ((f32[128,2,6,128]{3,1,2,0:T(2,128)}), f32[128,2,6,128]{3,1,2,0:T(2,128)S(1)}, u32[]{:S(2)}, u32[]{:S(2)}) async-start(f32[128,2,6,128]{3,1,2,0:T(2,128)} %copy.49), calls=%async_computation.2 | async-start | bytes 1572864 | tf_op jit(solution)/shard_map/all_to_all | solution.py:93
  126.0 61.2 %copy-start.1 = (s32[4,4,128]{2,1,0:T(4,128)S(1)}, s32[4,4,128]{2,1,0:T(4,128)}, u32[]{:S(2)}) copy-start(s32[4,4,128]{2,1,0:T(4,128)} %param.25) | copy-start | bytes 24580
  177.6 35.0 %all-to-all-start.3 = ((f32[128,2,3,128]{3,1,2,0:T(2,128)}), f32[128,2,3,128]{3,1,2,0:T(2,128)S(1)}, u32[]{:S(2)}, u32[]{:S(2)}) async-start(f32[128,2,3,128]{3,1,2,0:T(2,128)} %copy.52), calls=%async_computation.3 | async-start | bytes 786432 | tf_op jit(solution)/shard_map/all_to_all | solution.py:135
  187.1 487.2 %reduce-scatter.2.cloned.1.call-start = ((), (), s32[]{:S(2)}) async-start(), calls=%async_computation.5 | async-start | bytes 33816576 | tf_op jit(solution)/shard_map/reduce_scatter | solution.py:149
Sparse Core Ops, SparseCore 0:
  256.1 418.1 reduce-scatter.1
where the time goes:
time: 692 us; the launch traced here: 683 us
  waiting for transfers between devices  498 us (72%)
  other arithmetic  54 us (8%)
  blocking collectives  44.1 us (6%)
  matrix products  25.2 us (4%)
  starting transfers between devices  23.6 us (3%)
  local copies, waits for them, and re-layouts  22.5 us (3%)
  between operations  14.3 us (2%)
    reduce_scatter x1, waiting for transfers between devices, per_device(): lax.psum_scatter(running_partial_sum, 'tiles', scatter_dimension=1, tiled...  418 us
    all_to_all x1, waiting for transfers between devices, per_device(): lax.all_to_all(panel_geometry[asked], 'tiles', split_axis=0, concat_axis=...  39.4 us
    all_to_all x1, blocking collectives, per_device(): lax.all_to_all(wanted, 'tiles', split_axis=0, concat_axis=0, tiled=True)  35.1 us
    scatter-add x1, other arithmetic, per_device(): jnp.zeros((3, tile_count * vertex_width), jnp.float32).at[:, flat_ids]  24.6 us
    all_to_all x1, waiting for transfers between devices, per_device(): lax.all_to_all(table, 'tiles', split_axis=0, concat_axis=0, tiled=True)  23.9 us
    all_to_all x1, waiting for transfers between devices, per_device(): lax.all_to_all(strength_part[asked], 'tiles', split_axis=0, concat_axis=0...  16.8 us
  transfers between devices with their start and end apart: 4, of which 4 were waited for; matrix products, arithmetic and copies ran while one was open for 1% of the time, Pallas kernels for 0%

commit v1 on v0

v1 whole, which is shorter than its diff:
```python
import functools

import jax
import jax.numpy as jnp
from jax import lax
from jax.experimental import pallas as pl
from jax.experimental.pallas import tpu as pltpu
from jax.sharding import PartitionSpec as P

SLAB = 8
FAR = 4
PB = 128
PAIRS_DEV = 32
MESH = pl.DeviceIdType.MESH
F32 = jnp.float32
BF16 = jnp.bfloat16

ROOT_HALF = 0.5773502691896258
ROOT_FIFTH = 0.7745966692414834
RULES = {
    1: ((0.0, 1.0),),
    2: ((-ROOT_HALF, 0.5), (ROOT_HALF, 0.5)),
    3: ((0.0, 4.0 / 9.0), (-ROOT_FIFTH, 5.0 / 18.0), (ROOT_FIFTH, 5.0 / 18.0)),
}


def place(slabs):
    t = lax.axis_index("tiles")
    y = lax.axis_index("far")
    z = t // SLAB
    return t, z, t - z * SLAB, y, z % FAR


def send(src, dst, send_sem, recv_sem, device):
    pltpu.make_async_remote_copy(
        src_ref=src,
        dst_ref=dst,
        send_sem=send_sem,
        recv_sem=recv_sem,
        device_id=device,
        device_id_type=MESH,
    ).start()


def wait(ref, sem):
    pltpu.make_async_copy(ref, ref, sem).wait()


def gather_kernel(
    slabs,
    geom_ref,
    adj_ref,
    str_ref,
    tgt_ref,
    own_ref,
    src_ref,
    ord_ref,
    cnt_ref,
    sgeom_ref,
    sstr_ref,
    tadj_ref,
    tinfo_ref,
    codes_ref,
    send_sems,
    recv_sems,
):
    t, z, s, y, home = place(slabs)
    outer = slabs // FAR
    mine = y == home
    barrier = pltpu.get_barrier_semaphore()

    def greet(device):
        pl.semaphore_signal(barrier, inc=1, device_id=device, device_id_type=MESH)

    for zz in range(outer):
        for dy in range(1, FAR):
            yy = (home + dy) % FAR
            greet(((zz * FAR + y) * SLAB + s, yy))
    for dz in range(1, outer):
        greet(((((z // FAR + dz) % outer) * FAR + y) * SLAB + s, home))

    @pl.when(jnp.logical_not(mine))
    def _():
        greet((((z // FAR) * FAR + y) * SLAB + s, home))

    for ds in range(SLAB):
        for dy in range(FAR):
            if ds or dy:
                greet((z * SLAB + (s + ds) % SLAB, (y + dy) % FAR))

    tinfo_ref[s] = jnp.zeros((4, 8, PB), F32)
    for comp in range(3):
        for block in range(4):
            tinfo_ref[s, block, comp : comp + 1, :] = geom_ref[comp, block : block + 1, :]
    for row, ref in enumerate((tgt_ref, own_ref, src_ref, ord_ref)):
        tinfo_ref[s, 0, 3 + row : 4 + row, 0:PAIRS_DEV] = ref[...].astype(F32)
    slot = lax.broadcasted_iota(jnp.int32, (1, PB), 1)
    tinfo_ref[s, 0, 7:8, :] = jnp.where(slot < cnt_ref[0], 1.0, 0.0).astype(F32)

    pl.semaphore_wait(barrier, slabs + SLAB * FAR - 1 - mine.astype(jnp.int32))

    def send_source(zt, k):
        send(
            str_ref,
            sstr_ref.at[(z // FAR) * FAR + y],
            send_sems.at[0],
            recv_sems.at[0],
            (zt * SLAB + s, home),
        )

    for dz in range(1, slabs):
        send_source((z + dz) % slabs, 0)
    for dk in range(1, outer):
        zt = ((z // FAR + dk) % outer) * FAR + y
        send(
            geom_ref,
            sgeom_ref.at[z // FAR],
            send_sems.at[1],
            recv_sems.at[1],
            (zt * SLAB + s, home),
        )

    @pl.when(jnp.logical_not(mine))
    def _():
        send_source(z, 0)
        send(
            geom_ref,
            sgeom_ref.at[z // FAR],
            send_sems.at[1],
            recv_sems.at[1],
            (((z // FAR) * FAR + y) * SLAB + s, home),
        )

    @pl.when(mine)
    def _():
        sstr_ref[(z // FAR) * FAR + y] = str_ref[...]
        sgeom_ref[z // FAR] = geom_ref[...]

    for ds in range(1, SLAB):
        send(
            tinfo_ref.at[s],
            tinfo_ref.at[s],
            send_sems.at[3],
            recv_sems.at[3],
            (z * SLAB + (s + ds) % SLAB, y),
        )
    for ds in range(SLAB):
        for dy in range(FAR):
            if ds or dy:
                send(
                    adj_ref,
                    tadj_ref.at[s * FAR + y],
                    send_sems.at[2],
                    recv_sems.at[2],
                    (z * SLAB + (s + ds) % SLAB, (y + dy) % FAR),
                )
    tadj_ref[s * FAR + y] = adj_ref[...]

    wait(tinfo_ref.at[pl.ds(0, SLAB - 1)], recv_sems.at[3])
    codes_ref[...] = jnp.zeros((8, PB), jnp.int32)
    for k in range(SLAB):
        rows = tinfo_ref[k, 0].astype(jnp.int32)
        target, owner, source, order, live = (rows[r : r + 1] for r in range(3, 8))
        oz = owner // SLAB
        match = (
            (owner - oz * SLAB == s) & (oz - (oz // FAR) * FAR == y) & (live > 0) & (slot < PAIRS_DEV)
        )
        code = ((k * 4 + target) * 16 + (oz // FAR) * 4 + source) * 4 + order
        codes_ref[k : k + 1, :] = jnp.where(match, code, 0)

    wait(tadj_ref.at[pl.ds(0, SLAB * FAR - 1)], recv_sems.at[2])

    @pl.when(mine)
    def _():
        wait(sstr_ref.at[pl.ds(0, slabs - 1)], recv_sems.at[0])
        wait(sstr_ref.at[pl.ds(0, slabs - 1)], send_sems.at[0])
        if outer > 1:
            wait(sgeom_ref.at[pl.ds(0, outer - 1)], recv_sems.at[1])
            wait(sgeom_ref.at[pl.ds(0, outer - 1)], send_sems.at[1])

    @pl.when(jnp.logical_not(mine))
    def _():
        wait(sstr_ref.at[pl.ds(0, slabs)], recv_sems.at[0])
        wait(sstr_ref.at[pl.ds(0, slabs)], send_sems.at[0])
        wait(sgeom_ref.at[pl.ds(0, outer)], recv_sems.at[1])
        wait(sgeom_ref.at[pl.ds(0, outer)], send_sems.at[1])

    wait(tadj_ref.at[pl.ds(0, SLAB * FAR - 1)], send_sems.at[2])
    wait(tinfo_ref.at[pl.ds(0, SLAB - 1)], send_sems.at[3])


def pairs_kernel(
    slabs,
    codes_ref,
    sgeom_ref,
    sstr_ref,
    tadj_ref,
    tinfo_ref,
    source_ref,
    target_ref,
    s16_ref,
    t16_ref,
    tacc_ref,
    list_ref,
):
    outer = slabs // FAR

    def compact(k, n):
        row = k // (PAIRS_DEV // 8)
        column = (k - row * (PAIRS_DEV // 8)) * 8
        for i in range(8):
            code = codes_ref[row, column + i]
            list_ref[n] = code
            n = n + jnp.minimum(code, 1)
        return n

    total = lax.fori_loop(0, SLAB * PAIRS_DEV // 8, compact, jnp.int32(0))

    for a in range(outer):
        for yy in range(FAR):
            values = sstr_ref[a * FAR + yy].astype(F32)
            for j in range(4):
                s16_ref[a * 4 + j, 4 * yy : 4 * yy + 4, :] = values[4 * j : 4 * j + 4]
    for a in range(SLAB):
        for yy in range(FAR):
            values = tadj_ref[a * FAR + yy].astype(F32)
            for j in range(4):
                t16_ref[a * 4 + j, 4 * yy : 4 * yy + 4, :] = values[4 * j : 4 * j + 4]
    source_ref[...] = jnp.zeros(source_ref.shape, F32)
    tacc_ref[...] = jnp.zeros((PB, PB), F32)
    lane = lax.broadcasted_iota(jnp.int32, (1, PB), 1)

    def one_pair(i, carry):
        code = list_ref[i]
        order = code & 3
        source = (code >> 2) & 15
        target = code >> 6
        stack = jnp.concatenate([t16_ref[target], tinfo_ref[target // 4, target & 3]], axis=0)
        columns = stack.T
        coupling = jnp.dot(
            columns[:, 0:16].astype(BF16), s16_ref[source].astype(BF16), preferred_element_type=F32
        )
        centre = [columns[:, 16 + c : 17 + c] for c in range(3)]
        outer_index = source // 4
        block = source & 3
        base = [sgeom_ref[outer_index, c, pl.ds(block, 1), :] for c in range(3)]
        half = [0.25 * sgeom_ref[outer_index, 3 + c, pl.ds(block, 1), :] for c in range(3)]

        for rule, nodes in RULES.items():

            @pl.when(order == rule)
            def _():
                pulled = [None] * 3
                for node, weight in nodes:
                    differ = [
                        centre[c] - (base[c] + node * half[c] if node else base[c]) for c in range(3)
                    ]
                    squared = (
                        differ[0] * differ[0] + differ[1] * differ[1] + (differ[2] * differ[2] + 0.0625)
                    )
                    root = lax.rsqrt(squared)
                    factor = coupling * (root * root * root)
                    if weight != 1.0:
                        factor = factor * weight
                    for c in range(3):
                        term = factor * differ[c]
                        pulled[c] = term if pulled[c] is None else pulled[c] + term
                gathered = tacc_ref[...]
                for c in range(3):
                    source_ref[source, c : c + 1, :] += jnp.sum(pulled[c], axis=0, keepdims=True)
                    gathered = gathered - jnp.where(
                        lane == target * 4 + c, jnp.sum(pulled[c], axis=1, keepdims=True), 0.0
                    )
                tacc_ref[...] = gathered

        return carry

    lax.fori_loop(0, total, one_pair, 0)
    turned = tacc_ref[...].T
    for k in range(SLAB * 4):
        target_ref[k] = turned[4 * k : 4 * k + 4]


def scatter_kernel(
    slabs,
    source_ref,
    target_ref,
    corner_ref,
    out_ref,
    rs_source,
    rs_target,
    parts,
    landed,
    send_sems,
    recv_sems,
):
    t, z, s, y, home = place(slabs)
    outer = slabs // FAR
    tiles = slabs * SLAB
    mine = y == home
    barrier = pltpu.get_barrier_semaphore()

    def greet(device):
        pl.semaphore_signal(barrier, inc=1, device_id=device, device_id_type=MESH)

    for dz in range(1, slabs):
        greet((((z + dz) % slabs) * SLAB + s, home))

    @pl.when(jnp.logical_not(mine))
    def _():
        greet((z * SLAB + s, home))

    for ds in range(SLAB):
        for dy in range(FAR):
            if ds or dy:
                greet((z * SLAB + (s + ds) % SLAB, (y + dy) % FAR))
    shifts = (0, 1, tiles - 1, tiles // 2)
    for o in range(4):
        for dy in range(FAR):
            if o or dy:
                greet(((t + tiles - shifts[o]) % tiles, (y + dy) % FAR))

    vertex = corner_ref[y]
    holder = vertex // (4 * PB)
    away = holder - t
    away = jnp.where(away < 0, away + tiles, away)
    group = jnp.where(
        away == 0, 0, jnp.where(away == 1, 1, jnp.where(away == tiles - 1, 2, 3))
    )
    within = vertex - holder * (4 * PB)
    high = within // PB
    key = group * 4 + high
    low = within - high * PB
    row = lax.broadcasted_iota(jnp.int32, (PB, PB), 0)
    picks = jnp.concatenate(
        [jnp.where(row == low[j : j + 1], 1.0, 0.0).astype(BF16) for j in range(4)], axis=1
    )

    pl.semaphore_wait(barrier, slabs - mine.astype(jnp.int32) + SLAB * FAR - 1 + 15)

    def send_source(a, j):
        send(
            source_ref.at[a * 4 + j],
            rs_source.at[z],
            send_sems.at[0],
            recv_sems.at[0],
            ((a * FAR + y) * SLAB + s, j),
        )

    for da in range(outer):
        a = (z // FAR + da) % outer
        for dj in range(FAR):
            if dj:
                send_source(a, (y + dj) % FAR)
            elif da:
                send_source(a, y)

    @pl.when(jnp.logical_not(mine))
    def _():
        send_source(z // FAR, y)

    @pl.when(mine)
    def _():
        rs_source[z] = source_ref[(z // FAR) * 4 + y]

    for ds in range(SLAB):
        for dy in range(FAR):
            if ds or dy:
                st, yt = (s + ds) % SLAB, (y + dy) % FAR
                send(
                    target_ref.at[st * 4 + yt],
                    rs_target.at[s * FAR + y],
                    send_sems.at[1],
                    recv_sems.at[1],
                    (z * SLAB + st, yt),
                )
    rs_target[s * FAR + y] = target_ref[s * 4 + y]
    wait(rs_target.at[pl.ds(0, SLAB * FAR - 1)], recv_sems.at[1])

    @pl.when(mine)
    def _():
        wait(rs_source.at[pl.ds(0, slabs - 1)], recv_sems.at[0])

    @pl.when(jnp.logical_not(mine))
    def _():
        wait(rs_source.at[pl.ds(0, slabs)], recv_sems.at[0])

    grad = jnp.sum(rs_target[...], axis=0) + jnp.sum(rs_source[...], axis=0)
    grad = grad * (0.25 * 0.0078125)
    grad = jnp.concatenate([grad, grad], axis=0)
    wide = jnp.concatenate([grad] * 8, axis=0)
    rowkey = lax.broadcasted_iota(jnp.int32, (64, PB), 0) // 4
    first = wide.astype(BF16).astype(F32)
    second = wide - first
    spread = jnp.concatenate(
        [
            jnp.concatenate(
                [jnp.where(rowkey == key[j : j + 1], part, 0.0).astype(BF16) for j in range(4)], axis=1
            )
            for part in (first, second)
        ],
        axis=0,
    )
    sums = lax.dot_general(spread, picks, (((1,), (1,)), ((), ())), preferred_element_type=F32)
    sums = sums[0:64] + sums[64:128]
    for o in range(4):
        parts[o] = sums[16 * o : 16 * o + 16]
    for o in range(4):
        for dy in range(FAR):
            if o or dy:
                send(
                    parts.at[o],
                    landed.at[o * FAR + dy],
                    send_sems.at[2],
                    recv_sems.at[2],
                    ((t + shifts[o]) % tiles, (y + dy) % FAR),
                )
    landed[0] = parts[0]
    wait(landed.at[pl.ds(1, 15)], recv_sems.at[2])
    result = jnp.sum(landed[...], axis=0)
    for k in range(4):
        out_ref[:, k * PB : (k + 1) * PB] = result[4 * k : 4 * k + 3]

    wait(rs_target.at[pl.ds(0, SLAB * FAR - 1)], send_sems.at[1])

    @pl.when(mine)
    def _():
        wait(rs_source.at[pl.ds(0, slabs - 1)], send_sems.at[0])

    @pl.when(jnp.logical_not(mine))
    def _():
        wait(rs_source.at[pl.ds(0, slabs)], send_sems.at[0])

    wait(landed.at[pl.ds(1, 15)], send_sems.at[2])


def vmem():
    return pl.BlockSpec(memory_space=pltpu.VMEM)


def smem():
    return pl.BlockSpec(memory_space=pltpu.SMEM)


def shape(dims, dtype=F32):
    return jax.ShapeDtypeStruct(dims, dtype)


def per_device(
    panel_geometry,
    adjoint,
    strengths,
    pair_target,
    pair_owner,
    pair_source,
    pair_order,
    pair_count,
    corner_vertex,
):
    slabs = lax.axis_size("tiles") // SLAB
    outer = slabs // FAR
    row = lambda values: values.reshape(1, PAIRS_DEV)
    sgeom, sstr, tadj, tinfo, codes = pl.pallas_call(
        functools.partial(gather_kernel, slabs),
        out_shape=(
            shape((outer, 6, 4, PB)),
            shape((slabs, 16, PB), BF16),
            shape((SLAB * FAR, 16, PB), BF16),
            shape((SLAB, 4, 8, PB)),
            shape((8, PB), jnp.int32),
        ),
        in_specs=[vmem()] * 7 + [smem()],
        out_specs=(vmem(),) * 5,
        scratch_shapes=[pltpu.SemaphoreType.DMA((4,)), pltpu.SemaphoreType.DMA((4,))],
        compiler_params=pltpu.CompilerParams(collective_id=0, has_side_effects=True),
        name="gather_blocks",
    )(
        panel_geometry.transpose(1, 0, 2),
        adjoint.reshape(16, PB),
        strengths.reshape(16, PB),
        row(pair_target),
        row(pair_owner),
        row(pair_source),
        row(pair_order),
        pair_count,
    )
    source_grad, target_grad = pl.pallas_call(
        functools.partial(pairs_kernel, slabs),
        out_shape=(shape((outer * 4, 4, PB)), shape((SLAB * 4, 4, PB))),
        in_specs=[smem()] + [vmem()] * 4,
        out_specs=(vmem(),) * 2,
        scratch_shapes=[
            pltpu.VMEM((outer * 4, 16, PB), F32),
            pltpu.VMEM((SLAB * 4, 16, PB), F32),
            pltpu.VMEM((PB, PB), F32),
            pltpu.SMEM((SLAB * PAIRS_DEV + 8,), jnp.int32),
        ],
        name="pair_tiles",
    )(codes, sgeom, sstr, tadj, tinfo)
    return pl.pallas_call(
        functools.partial(scatter_kernel, slabs),
        out_shape=shape((3, 4 * PB)),
        in_specs=[vmem()] * 3,
        out_specs=vmem(),
        scratch_shapes=[
            pltpu.VMEM((slabs, 4, PB), F32),
            pltpu.VMEM((SLAB * FAR, 4, PB), F32),
            pltpu.VMEM((4, 16, PB), F32),
            pltpu.VMEM((16, 16, PB), F32),
            pltpu.SemaphoreType.DMA((3,)),
            pltpu.SemaphoreType.DMA((3,)),
        ],
        compiler_params=pltpu.CompilerParams(collective_id=1, has_side_effects=True),
        name="return_and_scatter",
    )(source_grad, target_grad, corner_vertex)


def solution(mesh):
    placed = (
        P("tiles", None, None),
        P("tiles", "far", None),
        P("tiles", "far", None),
        P("tiles"),
        P("tiles", None),
        P("tiles"),
        P("tiles"),
        P("tiles"),
        P("tiles", None, None),
    )
    return jax.shard_map(
        per_device, mesh=mesh, in_specs=placed, out_specs=P(None, "tiles"), check_vma=False
    )
```

time: 692 us -> 66.6 us (0.10)
  the two profiles are of different devices: /device:TPU:1 before, /device:TPU:2 now
where the time goes in v1:
time: 66.6 us; the launch traced here: 66.3 us
  Pallas kernels  64.4 us (97%)
  local copies, waits for them, and re-layouts  1.3 us (2%)
  between operations  0.67 us (1%)
    pallas_call x1, Pallas kernels, per_device(): pl.pallas_call(functools.partial(scatter_kernel, slabs), out_shape=shape(...  36.8 us
    pallas_call x1, Pallas kernels, per_device(): pl.pallas_call(functools.partial(gather_kernel, slabs), out_shape=(shape(...  24.2 us
    pallas_call x1, Pallas kernels, per_device(): pl.pallas_call(functools.partial(pairs_kernel, slabs), out_shape=(shape((...  3.41 us

profile of v1, /device:TPU:2, one launch (start us, length us, event | category | flops | bytes accessed | tf_op | source)
XLA Modules:
  0.0 66.3 jit_solution(15565680745914450408)
XLA Ops:
  0.7 24.2 %gather_blocks.1 = (f32[4,6,4,128]{3,2,1,0:T(4,128)}, bf16[16,16,128]{2,1,0:T(8,128)(2,1)}, bf16[32,16,128]{2,1,0:T(8,128)(2,1)}, f32[8,4,8,128]{3,2,1,0:T(8,128)}, s32[8,128]{1,0:T(8,128)}) custom-call(f32[6,4,128]{2,1,0:T(4,128)} %bitcast.7, bf16[16,128]{1,0:T(8,128)(2,1)} %bitcast.8, bf16[16,128]{1,0:T(8,128)(2,1)} %bitcast.9, s32[1,32]{1,0:T(1,128)} %bitcast.10, ...), custom_call_target="tpu_custom_call" | custom-call | tf_op jit(solution)/shard_map/gather_blocks/pallas_call | solution.py:463
  24.8 3.4 %pair_tiles.1 = (f32[16,4,128]{2,1,0:T(4,128)}, f32[32,4,128]{2,1,0:T(4,128)}) custom-call(s32[8,128]{1,0:T(8,128)} %get-tuple-element.12.codes_ref, f32[4,6,4,128]{3,2,1,0:T(4,128)} %get-tuple-element.13.sgeom_ref, bf16[16,16,128]{2,1,0:T(8,128)(2,1)} %get-tuple-element.14.sstr_ref, bf16[32,16,128]{2,1,0:T(8,128)(2,1)} %get-tuple-element.15.tadj_ref, ...), custom_call_target="tpu_custom_call" | custom-call | tf_op jit(solution)/shard_map/pair_tiles/pallas_call | solution.py:487
  28.2 36.8 %return_and_scatter.1 = f32[3,512]{1,0:T(4,128)} custom-call(f32[16,4,128]{2,1,0:T(4,128)} %get-tuple-element.17.source_ref, f32[32,4,128]{2,1,0:T(4,128)} %get-tuple-element.18.target_ref, s32[4,4,128]{2,1,0:T(4,128)} %corner_ref.1), custom_call_target="tpu_custom_call" | custom-call | tf_op jit(solution)/shard_map/return_and_scatter/pallas_call | solution.py:500
  65.0 1.3 %copy.12 = f32[3,512]{1,0:T(4,128)} copy(f32[3,512]{1,0:T(4,128)} %return_and_scatter.1) | data formatting | bytes 12288

commit v2 on v1

--- a/solution.py
+++ b/solution.py
@@ -83,10 +83,10 @@
     def _():
         greet((((z // FAR) * FAR + y) * SLAB + s, home))
 
-    for ds in range(SLAB):
-        for dy in range(FAR):
-            if ds or dy:
-                greet((z * SLAB + (s + ds) % SLAB, (y + dy) % FAR))
+    for ds in range(1, SLAB):
+        greet((z * SLAB + (s + ds) % SLAB, y))
+    for dy in range(1, FAR):
+        greet((t, (y + dy) % FAR))
 
     tinfo_ref[s] = jnp.zeros((4, 8, PB), F32)
     for comp in range(3):
@@ -97,7 +97,7 @@
     slot = lax.broadcasted_iota(jnp.int32, (1, PB), 1)
     tinfo_ref[s, 0, 7:8, :] = jnp.where(slot < cnt_ref[0], 1.0, 0.0).astype(F32)
 
-    pl.semaphore_wait(barrier, slabs + SLAB * FAR - 1 - mine.astype(jnp.int32))
+    pl.semaphore_wait(barrier, slabs - mine.astype(jnp.int32) + SLAB - 1 + FAR - 1)
 
     def send_source(zt, k):
         send(
@@ -136,6 +136,15 @@
         sstr_ref[(z // FAR) * FAR + y] = str_ref[...]
         sgeom_ref[z // FAR] = geom_ref[...]
 
+    for dy in range(1, FAR):
+        send(
+            adj_ref,
+            tadj_ref.at[s, y],
+            send_sems.at[2],
+            recv_sems.at[2],
+            (t, (y + dy) % FAR),
+        )
+    tadj_ref[s, y] = adj_ref[...]
     for ds in range(1, SLAB):
         send(
             tinfo_ref.at[s],
@@ -144,17 +153,15 @@
             recv_sems.at[3],
             (z * SLAB + (s + ds) % SLAB, y),
         )
-    for ds in range(SLAB):
-        for dy in range(FAR):
-            if ds or dy:
-                send(
-                    adj_ref,
-                    tadj_ref.at[s * FAR + y],
-                    send_sems.at[2],
-                    recv_sems.at[2],
-                    (z * SLAB + (s + ds) % SLAB, (y + dy) % FAR),
-                )
-    tadj_ref[s * FAR + y] = adj_ref[...]
+    wait(tadj_ref.at[s, pl.ds(0, FAR - 1)], recv_sems.at[2])
+    for ds in range(1, SLAB):
+        send(
+            tadj_ref.at[s],
+            tadj_ref.at[s],
+            send_sems.at[4],
+            recv_sems.at[4],
+            (z * SLAB + (s + ds) % SLAB, y),
+        )
 
     wait(tinfo_ref.at[pl.ds(0, SLAB - 1)], recv_sems.at[3])
     codes_ref[...] = jnp.zeros((8, PB), jnp.int32)
@@ -168,7 +175,7 @@
         code = ((k * 4 + target) * 16 + (oz // FAR) * 4 + source) * 4 + order
         codes_ref[k : k + 1, :] = jnp.where(match, code, 0)
 
-    wait(tadj_ref.at[pl.ds(0, SLAB * FAR - 1)], recv_sems.at[2])
+    wait(tadj_ref.at[pl.ds(0, SLAB - 1)], recv_sems.at[4])
 
     @pl.when(mine)
     def _():
@@ -185,7 +192,8 @@
         wait(sgeom_ref.at[pl.ds(0, outer)], recv_sems.at[1])
         wait(sgeom_ref.at[pl.ds(0, outer)], send_sems.at[1])
 
-    wait(tadj_ref.at[pl.ds(0, SLAB * FAR - 1)], send_sems.at[2])
+    wait(tadj_ref.at[s, pl.ds(0, FAR - 1)], send_sems.at[2])
+    wait(tadj_ref.at[pl.ds(0, SLAB - 1)], send_sems.at[4])
     wait(tinfo_ref.at[pl.ds(0, SLAB - 1)], send_sems.at[3])
 
 
@@ -202,19 +210,13 @@
     t16_ref,
     tacc_ref,
     list_ref,
+    codes,
+    codes_sem,
 ):
     outer = slabs // FAR
 
-    def compact(k, n):
-        row = k // (PAIRS_DEV // 8)
-        column = (k - row * (PAIRS_DEV // 8)) * 8
-        for i in range(8):
-            code = codes_ref[row, column + i]
-            list_ref[n] = code
-            n = n + jnp.minimum(code, 1)
-        return n
-
-    total = lax.fori_loop(0, SLAB * PAIRS_DEV // 8, compact, jnp.int32(0))
+    copy = pltpu.make_async_copy(codes_ref, codes, codes_sem)
+    copy.start()
 
     for a in range(outer):
         for yy in range(FAR):
@@ -223,12 +225,24 @@
                 s16_ref[a * 4 + j, 4 * yy : 4 * yy + 4, :] = values[4 * j : 4 * j + 4]
     for a in range(SLAB):
         for yy in range(FAR):
-            values = tadj_ref[a * FAR + yy].astype(F32)
+            values = tadj_ref[a, yy].astype(F32)
             for j in range(4):
                 t16_ref[a * 4 + j, 4 * yy : 4 * yy + 4, :] = values[4 * j : 4 * j + 4]
     source_ref[...] = jnp.zeros(source_ref.shape, F32)
     tacc_ref[...] = jnp.zeros((PB, PB), F32)
     lane = lax.broadcasted_iota(jnp.int32, (1, PB), 1)
+
+    def compact(k, n):
+        row = k // (PAIRS_DEV // 8)
+        column = (k - row * (PAIRS_DEV // 8)) * 8
+        for i in range(8):
+            code = codes[row, column + i]
+            list_ref[n] = code
+            n = n + jnp.minimum(code, 1)
+        return n
+
+    copy.wait()
+    total = lax.fori_loop(0, SLAB * PAIRS_DEV // 8, compact, jnp.int32(0))
 
     def one_pair(i, carry):
         code = list_ref[i]
@@ -267,9 +281,11 @@
                         pulled[c] = term if pulled[c] is None else pulled[c] + term
                 gathered = tacc_ref[...]
                 for c in range(3):
-                    source_ref[source, c : c + 1, :] += jnp.sum(pulled[c], axis=0, keepdims=True)
+                    source_ref[outer_index, c, pl.ds(block, 1), :] += jnp.sum(
+                        pulled[c], axis=0, keepdims=True
+                    )
                     gathered = gathered - jnp.where(
-                        lane == target * 4 + c, jnp.sum(pulled[c], axis=1, keepdims=True), 0.0
+                        lane == (target // 4) * 16 + c * 4 + (target & 3), jnp.sum(pulled[c], axis=1, keepdims=True), 0.0
                     )
                 tacc_ref[...] = gathered
 
@@ -277,8 +293,9 @@
 
     lax.fori_loop(0, total, one_pair, 0)
     turned = tacc_ref[...].T
-    for k in range(SLAB * 4):
-        target_ref[k] = turned[4 * k : 4 * k + 4]
+    for k in range(SLAB):
+        for c in range(3):
+            target_ref[k, c] = turned[16 * k + 4 * c : 16 * k + 4 * c + 4]
 
 
 def scatter_kernel(
@@ -298,114 +315,109 @@
     outer = slabs // FAR
     tiles = slabs * SLAB
     mine = y == home
+    base = (z // FAR) * FAR + y
     barrier = pltpu.get_barrier_semaphore()
 
     def greet(device):
         pl.semaphore_signal(barrier, inc=1, device_id=device, device_id_type=MESH)
 
-    for dz in range(1, slabs):
-        greet((((z + dz) % slabs) * SLAB + s, home))
-
-    @pl.when(jnp.logical_not(mine))
-    def _():
-        greet((z * SLAB + s, home))
-
-    for ds in range(SLAB):
-        for dy in range(FAR):
-            if ds or dy:
-                greet((z * SLAB + (s + ds) % SLAB, (y + dy) % FAR))
     shifts = (0, 1, tiles - 1, tiles // 2)
-    for o in range(4):
+    for o in (3, 1, 2, 0):
         for dy in range(FAR):
             if o or dy:
                 greet(((t + tiles - shifts[o]) % tiles, (y + dy) % FAR))
-
-    vertex = corner_ref[y]
-    holder = vertex // (4 * PB)
-    away = holder - t
-    away = jnp.where(away < 0, away + tiles, away)
-    group = jnp.where(
-        away == 0, 0, jnp.where(away == 1, 1, jnp.where(away == tiles - 1, 2, 3))
-    )
-    within = vertex - holder * (4 * PB)
-    high = within // PB
-    key = group * 4 + high
-    low = within - high * PB
+    for da in range(1, outer):
+        greet((((z // FAR + da) % outer * FAR + y) * SLAB + s, home))
+
+    @pl.when(jnp.logical_not(mine))
+    def _():
+        greet((base * SLAB + s, home))
+
+    for ds in range(1, SLAB):
+        greet((z * SLAB + (s + ds) % SLAB, y))
+
     row = lax.broadcasted_iota(jnp.int32, (PB, PB), 0)
-    picks = jnp.concatenate(
-        [jnp.where(row == low[j : j + 1], 1.0, 0.0).astype(BF16) for j in range(4)], axis=1
-    )
-
-    pl.semaphore_wait(barrier, slabs - mine.astype(jnp.int32) + SLAB * FAR - 1 + 15)
-
-    def send_source(a, j):
-        send(
-            source_ref.at[a * 4 + j],
-            rs_source.at[z],
+    picks = []
+    keys = []
+    for block in range(4):
+        vertex = corner_ref[block]
+        holder = vertex // (4 * PB)
+        away = holder - t
+        away = jnp.where(away < 0, away + tiles, away)
+        group = jnp.where(
+            away == 0, 0, jnp.where(away == 1, 1, jnp.where(away == tiles - 1, 2, 3))
+        )
+        within = vertex - holder * (4 * PB)
+        high = within // PB
+        low = within - high * PB
+        keys.append(group * 4 + high)
+        picks += [jnp.where(row == low[j : j + 1], 1.0, 0.0).astype(BF16) for j in range(4)]
+    picks = jnp.concatenate(picks, axis=1)
+
+    pl.semaphore_wait(barrier, 15 + outer - mine.astype(jnp.int32) + SLAB - 1)
+
+    def send_source(a):
+        send(
+            source_ref.at[a],
+            rs_source.at[z // FAR],
             send_sems.at[0],
             recv_sems.at[0],
-            ((a * FAR + y) * SLAB + s, j),
-        )
-
-    for da in range(outer):
-        a = (z // FAR + da) % outer
-        for dj in range(FAR):
-            if dj:
-                send_source(a, (y + dj) % FAR)
-            elif da:
-                send_source(a, y)
-
-    @pl.when(jnp.logical_not(mine))
-    def _():
-        send_source(z // FAR, y)
+            ((a * FAR + y) * SLAB + s, home),
+        )
+
+    for da in range(1, outer):
+        send_source((z // FAR + da) % outer)
+
+    @pl.when(jnp.logical_not(mine))
+    def _():
+        send_source(z // FAR)
 
     @pl.when(mine)
     def _():
-        rs_source[z] = source_ref[(z // FAR) * 4 + y]
-
-    for ds in range(SLAB):
-        for dy in range(FAR):
-            if ds or dy:
-                st, yt = (s + ds) % SLAB, (y + dy) % FAR
-                send(
-                    target_ref.at[st * 4 + yt],
-                    rs_target.at[s * FAR + y],
-                    send_sems.at[1],
-                    recv_sems.at[1],
-                    (z * SLAB + st, yt),
-                )
-    rs_target[s * FAR + y] = target_ref[s * 4 + y]
-    wait(rs_target.at[pl.ds(0, SLAB * FAR - 1)], recv_sems.at[1])
+        rs_source[z // FAR] = source_ref[z // FAR]
+
+    for ds in range(1, SLAB):
+        st = (s + ds) % SLAB
+        send(
+            target_ref.at[st],
+            rs_target.at[s],
+            send_sems.at[1],
+            recv_sems.at[1],
+            (z * SLAB + st, y),
+        )
+    rs_target[s] = target_ref[s]
+    wait(rs_target.at[pl.ds(0, SLAB - 1)], recv_sems.at[1])
 
     @pl.when(mine)
     def _():
-        wait(rs_source.at[pl.ds(0, slabs - 1)], recv_sems.at[0])
-
-    @pl.when(jnp.logical_not(mine))
-    def _():
-        wait(rs_source.at[pl.ds(0, slabs)], recv_sems.at[0])
+        if outer > 1:
+            wait(rs_source.at[pl.ds(0, outer - 1)], recv_sems.at[0])
+
+    @pl.when(jnp.logical_not(mine))
+    def _():
+        wait(rs_source.at[pl.ds(0, outer)], recv_sems.at[0])
 
     grad = jnp.sum(rs_target[...], axis=0) + jnp.sum(rs_source[...], axis=0)
     grad = grad * (0.25 * 0.0078125)
-    grad = jnp.concatenate([grad, grad], axis=0)
-    wide = jnp.concatenate([grad] * 8, axis=0)
-    rowkey = lax.broadcasted_iota(jnp.int32, (64, PB), 0) // 4
-    first = wide.astype(BF16).astype(F32)
-    second = wide - first
-    spread = jnp.concatenate(
-        [
-            jnp.concatenate(
-                [jnp.where(rowkey == key[j : j + 1], part, 0.0).astype(BF16) for j in range(4)], axis=1
-            )
-            for part in (first, second)
-        ],
-        axis=0,
-    )
+    rowkey = lax.broadcasted_iota(jnp.int32, (16, PB), 0)
+    upper = [[], [], []]
+    lower = [[], [], []]
+    for block in range(4):
+        for c in range(3):
+            wide = jnp.broadcast_to(grad[c, block : block + 1], (16, PB))
+            first = wide.astype(BF16)
+            second = (wide - first.astype(F32)).astype(BF16)
+            for j in range(4):
+                here = rowkey == keys[block][j : j + 1]
+                upper[c].append(jnp.where(here, first, jnp.zeros_like(first)))
+                lower[c].append(jnp.where(here, second, jnp.zeros_like(second)))
+    spread = jnp.concatenate([jnp.concatenate(part, axis=1) for part in upper + lower], axis=0)
     sums = lax.dot_general(spread, picks, (((1,), (1,)), ((), ())), preferred_element_type=F32)
-    sums = sums[0:64] + sums[64:128]
+    sums = sums[0:48] + sums[48:96]
     for o in range(4):
-        parts[o] = sums[16 * o : 16 * o + 16]
-    for o in range(4):
+        for c in range(3):
+            parts[o, c] = sums[16 * c + 4 * o : 16 * c + 4 * o + 4]
+    for o in (3, 1, 2, 0):
         for dy in range(FAR):
             if o or dy:
                 send(
@@ -419,23 +431,33 @@
     wait(landed.at[pl.ds(1, 15)], recv_sems.at[2])
     result = jnp.sum(landed[...], axis=0)
     for k in range(4):
-        out_ref[:, k * PB : (k + 1) * PB] = result[4 * k : 4 * k + 3]
-
-    wait(rs_target.at[pl.ds(0, SLAB * FAR - 1)], send_sems.at[1])
+        for c in range(3):
+            out_ref[c : c + 1, k * PB : (k + 1) * PB] = result[c, k : k + 1]
+
+    wait(rs_target.at[pl.ds(0, SLAB - 1)], send_sems.at[1])
 
     @pl.when(mine)
     def _():
-        wait(rs_source.at[pl.ds(0, slabs - 1)], send_sems.at[0])
-
-    @pl.when(jnp.logical_not(mine))
-    def _():
-        wait(rs_source.at[pl.ds(0, slabs)], send_sems.at[0])
+        if outer > 1:
+            wait(rs_source.at[pl.ds(0, outer - 1)], send_sems.at[0])
+
+    @pl.when(jnp.logical_not(mine))
+    def _():
+        wait(rs_source.at[pl.ds(0, outer)], send_sems.at[0])
 
     wait(landed.at[pl.ds(1, 15)], send_sems.at[2])
 
 
 def vmem():
     return pl.BlockSpec(memory_space=pltpu.VMEM)
+
+
+def resident(dims, dtype):
+    return pltpu.VMEM(dims, dtype)
+
+
+def held(*arrays):
+    return [pltpu.with_memory_space_constraint(a, pltpu.VMEM) for a in arrays]
 
 
 def smem():
@@ -463,15 +485,15 @@
     sgeom, sstr, tadj, tinfo, codes = pl.pallas_call(
         functools.partial(gather_kernel, slabs),
         out_shape=(
-            shape((outer, 6, 4, PB)),
-            shape((slabs, 16, PB), BF16),
-            shape((SLAB * FAR, 16, PB), BF16),
-            shape((SLAB, 4, 8, PB)),
-            shape((8, PB), jnp.int32),
+            resident((outer, 6, 4, PB), F32),
+            resident((slabs, 16, PB), BF16),
+            resident((SLAB, FAR, 16, PB), BF16),
+            resident((SLAB, 4, 8, PB), F32),
+            resident((8, PB), jnp.int32),
         ),
         in_specs=[vmem()] * 7 + [smem()],
         out_specs=(vmem(),) * 5,
-        scratch_shapes=[pltpu.SemaphoreType.DMA((4,)), pltpu.SemaphoreType.DMA((4,))],
+        scratch_shapes=[pltpu.SemaphoreType.DMA((5,)), pltpu.SemaphoreType.DMA((5,))],
         compiler_params=pltpu.CompilerParams(collective_id=0, has_side_effects=True),
         name="gather_blocks",
     )(
@@ -486,33 +508,35 @@
     )
     source_grad, target_grad = pl.pallas_call(
         functools.partial(pairs_kernel, slabs),
-        out_shape=(shape((outer * 4, 4, PB)), shape((SLAB * 4, 4, PB))),
-        in_specs=[smem()] + [vmem()] * 4,
+        out_shape=(resident((outer, 3, 4, PB), F32), resident((SLAB, 3, 4, PB), F32)),
+        in_specs=[vmem()] * 5,
         out_specs=(vmem(),) * 2,
         scratch_shapes=[
             pltpu.VMEM((outer * 4, 16, PB), F32),
             pltpu.VMEM((SLAB * 4, 16, PB), F32),
             pltpu.VMEM((PB, PB), F32),
             pltpu.SMEM((SLAB * PAIRS_DEV + 8,), jnp.int32),
+            pltpu.SMEM((8, PB), jnp.int32),
+            pltpu.SemaphoreType.DMA,
         ],
         name="pair_tiles",
-    )(codes, sgeom, sstr, tadj, tinfo)
+    )(*held(codes, sgeom, sstr, tadj, tinfo))
     return pl.pallas_call(
         functools.partial(scatter_kernel, slabs),
         out_shape=shape((3, 4 * PB)),
         in_specs=[vmem()] * 3,
         out_specs=vmem(),
         scratch_shapes=[
-            pltpu.VMEM((slabs, 4, PB), F32),
-            pltpu.VMEM((SLAB * FAR, 4, PB), F32),
-            pltpu.VMEM((4, 16, PB), F32),
-            pltpu.VMEM((16, 16, PB), F32),
+            pltpu.VMEM((outer, 3, 4, PB), F32),
+            pltpu.VMEM((SLAB, 3, 4, PB), F32),
+            pltpu.VMEM((4, 3, 4, PB), F32),
+            pltpu.VMEM((16, 3, 4, PB), F32),
             pltpu.SemaphoreType.DMA((3,)),
             pltpu.SemaphoreType.DMA((3,)),
         ],
         compiler_params=pltpu.CompilerParams(collective_id=1, has_side_effects=True),
         name="return_and_scatter",
-    )(source_grad, target_grad, corner_vertex)
+    )(*held(source_grad, target_grad), corner_vertex)
 
 
 def solution(mesh):

time: 66.6 us -> 63.8 us (0.958)
  Pallas kernels: 64.4 us -> 61.5 us
    pallas_call x1, Pallas kernels: 36.8 us -> 30.9 us  [per_device(): pl.pallas_call(functools.partial(scatter_kernel, slabs), out_shape=shape(...]
    pallas_call x2, Pallas kernels: 27.6 us -> 30.7 us  [the longest x1 23.9 us: per_device(): pl.pallas_call(functools.partial(gather_kernel, slabs), out_shape=(reside...]
where the time goes in v2:
time: 63.8 us; the launch traced here: 63.5 us
  Pallas kernels  61.5 us (96%)
  local copies, waits for them, and re-layouts  1.3 us (2%)
  between operations  0.68 us (1%)
    pallas_call x1, Pallas kernels, per_device(): pl.pallas_call(functools.partial(scatter_kernel, slabs), out_shape=shape(...  30.9 us
    pallas_call x1, Pallas kernels, per_device(): pl.pallas_call(functools.partial(gather_kernel, slabs), out_shape=(reside...  23.9 us
    pallas_call x1, Pallas kernels, per_device(): pl.pallas_call(functools.partial(pairs_kernel, slabs), out_shape=(residen...  6.82 us
    unnamed x1, local copies, waits for them, and re-layouts  1.3 us

profile of v2, /device:TPU:2, one launch (start us, length us, event | category | flops | bytes accessed | tf_op | source)
XLA Modules:
  0.0 63.5 jit_solution(6808855667248783199)
XLA Ops:
  0.7 23.9 %gather_blocks.1 = (f32[4,6,4,128]{3,2,1,0:T(4,128)S(1)}, bf16[16,16,128]{2,1,0:T(8,128)(2,1)S(1)}, bf16[8,4,16,128]{3,2,1,0:T(8,128)(2,1)S(1)}, f32[8,4,8,128]{3,2,1,0:T(8,128)S(1)}, s32[8,128]{1,0:T(8,128)S(1)}) custom-call(f32[6,4,128]{2,1,0:T(4,128)} %bitcast.7, bf16[16,128]{1,0:T(8,128)(2,1)} %bitcast.8, bf16[16,128]{1,0:T(8,128)(2,1)} %bitcast.9, ...), custom_call_target="tpu_custom_call" | custom-call | tf_op jit(solution)/shard_map/gather_blocks/pallas_call | solution.py:485
  24.5 6.8 %pair_tiles.1 = (f32[4,3,4,128]{3,2,1,0:T(4,128)S(1)}, f32[8,3,4,128]{3,2,1,0:T(4,128)S(1)}) custom-call(s32[8,128]{1,0:T(8,128)S(1)} %get-tuple-element.12.codes_ref, f32[4,6,4,128]{3,2,1,0:T(4,128)S(1)} %get-tuple-element.13.sgeom_ref, bf16[16,16,128]{2,1,0:T(8,128)(2,1)S(1)} %get-tuple-element.14.sstr_ref, ...), custom_call_target="tpu_custom_call" | custom-call | tf_op jit(solution)/shard_map/pair_tiles/pallas_call | solution.py:509
  31.4 30.9 %return_and_scatter.1 = f32[3,512]{1,0:T(4,128)} custom-call(f32[4,3,4,128]{3,2,1,0:T(4,128)S(1)} %get-tuple-element.17.source_ref, f32[8,3,4,128]{3,2,1,0:T(4,128)S(1)} %get-tuple-element.18.target_ref, s32[4,4,128]{2,1,0:T(4,128)} %corner_ref.1), custom_call_target="tpu_custom_call" | custom-call | tf_op jit(solution)/shard_map/return_and_scatter/pallas_call | solution.py:524
  62.2 1.3 %copy.12 = f32[3,512]{1,0:T(4,128)} copy(f32[3,512]{1,0:T(4,128)} %return_and_scatter.1) | data formatting | bytes 12288

commit v3 on v0

v3 whole, which is shorter than its diff:
```python
import functools

import jax
import jax.numpy as jnp
from jax import lax
from jax.experimental import pallas as pl
from jax.experimental.pallas import tpu as pltpu
from jax.sharding import PartitionSpec as P

SLAB = 8
FAR = 4
PB = 128
PAIRS_DEV = 32
MESH = pl.DeviceIdType.MESH
F32 = jnp.float32
BF16 = jnp.bfloat16

ROOT_HALF = 0.5773502691896258
ROOT_FIFTH = 0.7745966692414834
WITHIN = 4 * PB
def place(slabs):
    t = lax.axis_index("tiles")
    y = lax.axis_index("far")
    z = t // SLAB
    return t, z, t - z * SLAB, y, z % FAR


def send(src, dst, send_sem, recv_sem, device):
    pltpu.make_async_remote_copy(
        src_ref=src,
        dst_ref=dst,
        send_sem=send_sem,
        recv_sem=recv_sem,
        device_id=device,
        device_id_type=MESH,
    ).start()


def wait(ref, sem):
    pltpu.make_async_copy(ref, ref, sem).wait()


def split(values):
    high = values.astype(BF16).astype(F32)
    rest = values - high
    middle = rest.astype(BF16).astype(F32)
    return high, middle, (rest - middle).astype(BF16).astype(F32)


def squares(points, offset):
    total = points[0:1] * points[0:1] + points[1:2] * points[1:2] + (points[2:3] * points[2:3] + offset)
    return split(total)


def kernel(
    slabs,
    geom_ref,
    adj_ref,
    str_ref,
    tgt_ref,
    own_ref,
    src_ref,
    ord_ref,
    cnt_ref,
    corner_ref,
    out_ref,
    sgeom,
    sstr,
    tadj,
    tinfo,
    left,
    trow,
    sbase,
    srow,
    right,
    right_far,
    source_acc,
    target_acc,
    rs_source,
    rs_target,
    parts,
    landed,
    codes_v,
    codes,
    codes_sem,
    str_sems,
    geom_sems,
    send_sems,
    recv_sems,
):
    t, z, s, y, home = place(slabs)
    outer = slabs // FAR
    quarter = z // FAR
    tiles = slabs * SLAB
    mine = y == home
    other = jnp.logical_not(mine)
    barrier = pltpu.get_barrier_semaphore()
    near_first = {1: (0,), 2: (0, 1), 4: (0, 1, 3, 2)}[outer]
    shifts = (0, 1, tiles - 1, tiles // 2)

    def greet(device):
        pl.semaphore_signal(barrier, inc=1, device_id=device, device_id_type=MESH)

    for zz in range(outer):
        for dy in range(1, FAR):
            greet(((zz * FAR + y) * SLAB + s, (home + dy) % FAR))
    for dz in range(1, outer):
        greet(((((quarter + dz) % outer) * FAR + y) * SLAB + s, home))

    @pl.when(other)
    def _():
        greet(((quarter * FAR + y) * SLAB + s, home))

    for o in (3, 1, 2, 0):
        for dy in range(FAR):
            if o or dy:
                greet(((t + tiles - shifts[o]) % tiles, (y + dy) % FAR))
    for ds in range(1, SLAB):
        greet((z * SLAB + (s + ds) % SLAB, y))

    lane = lax.broadcasted_iota(jnp.int32, (1, PB), 1)
    tinfo[s] = jnp.zeros((4, 8, PB), F32)
    for comp in range(3):
        for block in range(4):
            tinfo[s, block, comp : comp + 1, :] = geom_ref[comp, block : block + 1, :]
    live = lax.broadcasted_iota(jnp.int32, (1, PAIRS_DEV), 1) < cnt_ref[0]
    orders = jnp.where(live, ord_ref[...], 0)
    for row, values in enumerate((tgt_ref[...], own_ref[...], src_ref[...], orders)):
        tinfo[s, 0, 4 + row : 5 + row, 0:PAIRS_DEV] = values.astype(F32)

    pl.semaphore_wait(barrier, slabs - mine.astype(jnp.int32) + SLAB - 1 + 15)

    def send_strengths(zt):
        da = (quarter - zt // FAR + outer) % outer
        send(str_ref, sstr.at[da, y], send_sems.at[0], str_sems.at[da], (zt * SLAB + s, home))

    def send_geometry(zt):
        da = (quarter - zt // FAR + outer) % outer
        send(geom_ref, sgeom.at[da], send_sems.at[1], geom_sems.at[da], (zt * SLAB + s, home))

    for step in range(slabs // 2, 0, -1):
        send_strengths((z + step) % slabs)
        if 2 * step != slabs:
            send_strengths((z + slabs - step) % slabs)
    for dk in near_first[::-1]:
        if dk:
            send_geometry(((quarter + dk) % outer) * FAR + y)

    @pl.when(other)
    def _():
        send_strengths(z)
        send_geometry(quarter * FAR + y)

    @pl.when(mine)
    def _():
        sstr[0, y] = str_ref[...]
        sgeom[0] = geom_ref[...]

    for dy in range(1, FAR):
        send(adj_ref, tadj.at[s, y], send_sems.at[2], recv_sems.at[2], (t, (y + dy) % FAR))
    for ds in range(1, SLAB):
        peer = (z * SLAB + (s + ds) % SLAB, y)
        send(tinfo.at[s], tinfo.at[s], send_sems.at[3], recv_sems.at[3], peer)
    tadj[s, y] = adj_ref[...]
    wait(tadj.at[s, pl.ds(0, FAR - 1)], recv_sems.at[2])
    for ds in range(1, SLAB):
        peer = (z * SLAB + (s + ds) % SLAB, y)
        send(tadj.at[s], tadj.at[s], send_sems.at[4], recv_sems.at[4], peer)

    row = lax.broadcasted_iota(jnp.int32, (PB, PB), 0)
    picks = []
    keys = []
    for block in range(4):
        vertex = corner_ref[block]
        holder = vertex // (4 * PB)
        away = holder - t
        away = jnp.where(away < 0, away + tiles, away)
        group = jnp.where(
            away == 0, 0, jnp.where(away == 1, 1, jnp.where(away == tiles - 1, 2, 3))
        )
        within = vertex - holder * (4 * PB)
        high = within // PB
        low = within - high * PB
        keys.append(group * 4 + high)
        picks += [jnp.where(row == low[j : j + 1], 1.0, 0.0).astype(BF16) for j in range(4)]
    picks = jnp.concatenate(picks, axis=1)

    wait(tinfo.at[pl.ds(0, SLAB - 1)], recv_sems.at[3])
    place_of = lax.broadcasted_iota(jnp.int32, (8, PB), 0)
    wide_lane = lax.broadcasted_iota(jnp.int32, (8, PB), 1)
    da_of = place_of // 2
    wanted = ((quarter + da_of) % outer * FAR + y) * SLAB + s
    before = jnp.where(
        lax.broadcasted_iota(jnp.int32, (PB, PB), 0) < lax.broadcasted_iota(jnp.int32, (PB, PB), 1), 1.0, 0.0
    ).astype(BF16)
    for k in range(SLAB):
        rows = tinfo[k, 0].astype(jnp.int32)
        target, owner, source, order = (rows[r : r + 1] for r in range(4, 8))
        match = (owner == wanted) & (order > 0) & (wide_lane < PAIRS_DEV) & (da_of < outer)
        count = jnp.dot(
            jnp.where(match, 1.0, 0.0).astype(BF16), before, preferred_element_type=F32
        ).astype(jnp.int32)
        code = (target * 4 + source) * 4 + order
        chosen = jnp.where(match & (count == place_of - 2 * da_of), code, 0).astype(F32)
        total = jnp.sum(chosen, axis=1, keepdims=True).astype(jnp.int32)
        codes_v[k] = jnp.broadcast_to(total, (8, PB))
    copy = pltpu.make_async_copy(codes_v, codes, codes_sem)
    copy.start()

    wait(tadj.at[pl.ds(0, SLAB - 1)], recv_sems.at[4])
    zero4 = jnp.zeros((4, PB), F32)
    one = jnp.ones((1, PB), F32)
    zero1 = jnp.zeros((1, PB), F32)

    def prepare_list(k, carry):
        conditions = [tadj[k, yy].astype(F32) for yy in range(FAR)]
        for block in range(4):
            centre = tinfo[k, block][0:4]
            high, middle, low = split(centre)
            sq = squares(centre, 0.0)
            stack = jnp.concatenate(
                [c[4 * block : 4 * block + 4] for c in conditions]
                + [high, high, high, middle, middle, low]
                + [*sq, one, one, one, zero1, zero1],
                axis=0,
            )
            left[k * 4 + block] = stack.T.astype(BF16)
            trow[k * 4 + block] = jnp.concatenate(
                [one, zero1, zero1, zero1, high, middle, low], axis=0
            ).astype(BF16)
        target_acc[k] = jnp.zeros((4, 4, PB), F32)
        return carry

    lax.fori_loop(0, SLAB, prepare_list, 0)
    copy.wait()

    for da in near_first:
        if da:
            wait(sstr.at[da], str_sems.at[da])
            wait(sgeom.at[da], geom_sems.at[da])
        else:

            @pl.when(mine)
            def _():
                wait(sstr.at[0, pl.ds(0, FAR - 1)], str_sems.at[0])

            @pl.when(other)
            def _():
                wait(sstr.at[0], str_sems.at[0])
                wait(sgeom.at[0], geom_sems.at[0])

        conditions = [sstr[da, yy].astype(F32) for yy in range(FAR)]
        for block in range(4):
            base = jnp.concatenate([sgeom[da, c, block : block + 1, :] for c in range(3)] + [zero1], axis=0)
            half = 0.25 * jnp.concatenate(
                [sgeom[da, 3 + c, block : block + 1, :] for c in range(3)] + [zero1], axis=0
            )
            sbase[block] = jnp.concatenate([base, half], axis=0)
            first, second = split(base), split(half)
            srow[block] = jnp.concatenate(
                [
                    jnp.concatenate([one, zero1, zero1, zero1, *first], axis=0),
                    jnp.concatenate([zero4, *second], axis=0),
                ],
                axis=1,
            ).astype(BF16)

            def distance(points):
                high, middle, low = (-2.0 * part for part in split(points))
                sq = squares(points, 0.0625)
                return jnp.concatenate(
                    [zero4] * 4
                    + [high, middle, low, high, middle, high]
                    + [one, one, one, *sq, zero1, zero1],
                    axis=0,
                )

            coupled = jnp.concatenate(
                [c[4 * block : 4 * block + 4] for c in conditions] + [zero4] * 8, axis=0
            )
            right[block] = jnp.concatenate([coupled, distance(base)], axis=1).astype(BF16)
            for rule, node in enumerate((ROOT_HALF, ROOT_FIFTH)):
                right_far[block * 2 + rule] = jnp.concatenate(
                    [distance(base + node * half), distance(base - node * half)], axis=1
                ).astype(BF16)
        source_acc[da] = jnp.zeros((4, 4, PB), F32)

        def one_list(k, carry, da=da):
            for occurrence in range(2):
                code = codes[k, 2 * da + occurrence, 0]
                order = code & 3
                source = (code >> 2) & 3
                target = (code >> 4) & 3
                centre_weight = jnp.where(order == 1, 1.0, jnp.where(order == 3, 4.0 / 9.0, 0.0))
                side_weight = jnp.where(order == 2, 0.5, jnp.where(order == 3, 5.0 / 18.0, 0.0))
                shift_weight = jnp.where(
                    order == 2, 0.5 * ROOT_HALF, jnp.where(order == 3, 5.0 / 18.0 * ROOT_FIFTH, 0.0)
                )
                columns = left[k * 4 + target]
                inner = jnp.dot(columns, right[source], preferred_element_type=F32)
                sides = jnp.dot(columns, right_far[source * 2 + ((order + 1) >> 2)], preferred_element_type=F32)
                roots = lax.rsqrt(inner[:, PB:])
                pulls = lax.rsqrt(sides)
                roots = roots * roots * roots
                pulls = pulls * pulls * pulls
                coupling = inner[:, :PB]
                plus, minus = pulls[:, :PB], pulls[:, PB:]
                both = coupling * (centre_weight * roots + side_weight * (plus + minus))
                skew = (shift_weight * coupling) * (plus - minus)
                high = jnp.concatenate([both.astype(BF16), skew.astype(BF16)], axis=1)
                low = jnp.concatenate(
                    [
                        (both - high[:, :PB].astype(F32)).astype(BF16),
                        (skew - high[:, PB:].astype(F32)).astype(BF16),
                    ],
                    axis=1,
                )
                rows = trow[k * 4 + target]
                by_source = jnp.dot(rows, high, preferred_element_type=F32) + jnp.dot(
                    rows, low, preferred_element_type=F32
                )
                lines = srow[source]
                across = (((1,), (1,)), ((), ()))
                by_target = lax.dot_general(
                    lines, high, across, preferred_element_type=F32
                ) + lax.dot_general(lines, low, across, preferred_element_type=F32)
                points = sbase[source]
                pulled = (
                    by_source[4:8, :PB]
                    + by_source[8:12, :PB]
                    + by_source[12:16, :PB]
                    - points[0:4] * by_source[0:1, :PB]
                    - points[4:8] * by_source[0:1, PB:]
                )
                pushed = (
                    by_target[4:8]
                    + by_target[8:12]
                    + by_target[12:16]
                    - tinfo[k, target][0:4] * by_target[0:1]
                )
                for block in range(4):
                    source_acc[da, block] += jnp.where(source == block, 1.0, 0.0) * pulled
                    target_acc[k, block] += jnp.where(target == block, 1.0, 0.0) * pushed
            return carry

        lax.fori_loop(0, SLAB, one_list, 0)

        def send_source(da=da):
            send(
                source_acc.at[da],
                rs_source.at[quarter],
                send_sems.at[5],
                recv_sems.at[5],
                ((((quarter + da) % outer) * FAR + y) * SLAB + s, home),
            )

        if da:
            send_source()
        else:
            pl.when(other)(send_source)

            @pl.when(mine)
            def _():
                rs_source[quarter] = source_acc[0]

    for ds in range(1, SLAB):
        st = (s + ds) % SLAB
        send(target_acc.at[st], rs_target.at[s], send_sems.at[6], recv_sems.at[6], (z * SLAB + st, y))
    rs_target[s] = target_acc[s]
    wait(rs_target.at[pl.ds(0, SLAB - 1)], recv_sems.at[6])

    @pl.when(mine)
    def _():
        if outer > 1:
            wait(rs_source.at[pl.ds(0, outer - 1)], recv_sems.at[5])

    @pl.when(other)
    def _():
        wait(rs_source.at[pl.ds(0, outer)], recv_sems.at[5])

    grad = jnp.sum(rs_target[...], axis=0) + jnp.sum(rs_source[...], axis=0)
    grad = grad * (0.25 * 0.0078125)
    rowkey = lax.broadcasted_iota(jnp.int32, (16, PB), 0)
    upper = [[], [], []]
    lower = [[], [], []]
    for block in range(4):
        for c in range(3):
            wide = jnp.broadcast_to(grad[block, c : c + 1], (16, PB))
            first = wide.astype(BF16)
            second = (wide - first.astype(F32)).astype(BF16)
            for j in range(4):
                here = rowkey == keys[block][j : j + 1]
                upper[c].append(jnp.where(here, first, jnp.zeros_like(first)))
                lower[c].append(jnp.where(here, second, jnp.zeros_like(second)))
    spread = jnp.concatenate([jnp.concatenate(part, axis=1) for part in upper + lower], axis=0)
    sums = lax.dot_general(spread, picks, (((1,), (1,)), ((), ())), preferred_element_type=F32)
    sums = sums[0:48] + sums[48:96]
    for o in range(4):
        for c in range(3):
            parts[o, c] = sums[16 * c + 4 * o : 16 * c + 4 * o + 4]
    for o in (3, 1, 2, 0):
        for dy in range(FAR):
            if o or dy:
                send(
                    parts.at[o],
                    landed.at[o * FAR + dy],
                    send_sems.at[7],
                    recv_sems.at[7],
                    ((t + shifts[o]) % tiles, (y + dy) % FAR),
                )
    landed[0] = parts[0]
    wait(landed.at[pl.ds(1, 15)], recv_sems.at[7])
    result = jnp.sum(landed[...], axis=0)
    for k in range(4):
        for c in range(3):
            out_ref[c : c + 1, k * PB : (k + 1) * PB] = result[c, k : k + 1]

    wait(tadj.at[s, pl.ds(0, FAR - 1)], send_sems.at[2])
    wait(tinfo.at[pl.ds(0, SLAB - 1)], send_sems.at[3])
    wait(tadj.at[pl.ds(0, SLAB - 1)], send_sems.at[4])
    wait(rs_target.at[pl.ds(0, SLAB - 1)], send_sems.at[6])
    wait(landed.at[pl.ds(1, 15)], send_sems.at[7])

    @pl.when(mine)
    def _():
        if outer > 1:
            wait(sstr.at[pl.ds(0, outer - 1)], send_sems.at[0])
            wait(sgeom.at[pl.ds(0, outer - 1)], send_sems.at[1])
            wait(rs_source.at[pl.ds(0, outer - 1)], send_sems.at[5])
        wait(sstr.at[0, pl.ds(0, FAR - 1)], send_sems.at[0])

    @pl.when(other)
    def _():
        wait(sstr, send_sems.at[0])
        wait(sgeom, send_sems.at[1])
        wait(rs_source, send_sems.at[5])


def vmem():
    return pl.BlockSpec(memory_space=pltpu.VMEM)


def smem():
    return pl.BlockSpec(memory_space=pltpu.SMEM)


def per_device(
    panel_geometry,
    adjoint,
    strengths,
    pair_target,
    pair_owner,
    pair_source,
    pair_order,
    pair_count,
    corner_vertex,
):
    slabs = lax.axis_size("tiles") // SLAB
    outer = slabs // FAR
    row = lambda values: values.reshape(1, PAIRS_DEV)
    return pl.pallas_call(
        functools.partial(kernel, slabs),
        out_shape=jax.ShapeDtypeStruct((3, WITHIN), F32),
        in_specs=[vmem()] * 7 + [smem(), vmem()],
        out_specs=vmem(),
        scratch_shapes=[
            pltpu.VMEM((outer, 6, 4, PB), F32),
            pltpu.VMEM((outer, FAR, 16, PB), BF16),
            pltpu.VMEM((SLAB, FAR, 16, PB), BF16),
            pltpu.VMEM((SLAB, 4, 8, PB), F32),
            pltpu.VMEM((SLAB * 4, PB, 48), BF16),
            pltpu.VMEM((SLAB * 4, 16, PB), BF16),
            pltpu.VMEM((4, 8, PB), F32),
            pltpu.VMEM((4, 16, 2 * PB), BF16),
            pltpu.VMEM((4, 48, 2 * PB), BF16),
            pltpu.VMEM((8, 48, 2 * PB), BF16),
            pltpu.VMEM((outer, 4, 4, PB), F32),
            pltpu.VMEM((SLAB, 4, 4, PB), F32),
            pltpu.VMEM((outer, 4, 4, PB), F32),
            pltpu.VMEM((SLAB, 4, 4, PB), F32),
            pltpu.VMEM((4, 3, 4, PB), F32),
            pltpu.VMEM((16, 3, 4, PB), F32),
            pltpu.VMEM((SLAB, 8, PB), jnp.int32),
            pltpu.SMEM((SLAB, 8, PB), jnp.int32),
            pltpu.SemaphoreType.DMA,
            pltpu.SemaphoreType.DMA((outer,)),
            pltpu.SemaphoreType.DMA((outer,)),
            pltpu.SemaphoreType.DMA((8,)),
            pltpu.SemaphoreType.DMA((8,)),
        ],
        compiler_params=pltpu.CompilerParams(
            collective_id=0, has_side_effects=True, vmem_limit_bytes=48 * 1024 * 1024
        ),
        name="gather_pairs_return",
    )(
        panel_geometry.transpose(1, 0, 2),
        adjoint.reshape(16, PB),
        strengths.reshape(16, PB),
        row(pair_target),
        row(pair_owner),
        row(pair_source),
        row(pair_order),
        pair_count,
        corner_vertex,
    )


def solution(mesh):
    placed = (
        P("tiles", None, None),
        P("tiles", "far", None),
        P("tiles", "far", None),
        P("tiles"),
        P("tiles", None),
        P("tiles"),
        P("tiles"),
        P("tiles"),
        P("tiles", None, None),
    )
    return jax.shard_map(
        per_device, mesh=mesh, in_specs=placed, out_specs=P(None, "tiles"), check_vma=False
    )
```

time: 692 us -> 65.4 us (0.09); the launches traced: 683 us -> 64.9 us
  waiting for transfers between devices: 498 us -> 0 us
  Pallas kernels: 0 us -> 60.9 us
  other arithmetic: 54 us -> 0 us
  blocking collectives: 44.1 us -> 0 us
  matrix products: 25.2 us -> 0 us
  starting transfers between devices: 23.6 us -> 0 us
  local copies, waits for them, and re-layouts: 22.5 us -> 3.33 us
  between operations: 14.3 us -> 0.72 us
    reduce_scatter x1 -> x0, waiting for transfers between devices: 418 us -> none  [per_device(): lax.psum_scatter(running_partial_sum, 'tiles', scatter_dimension=1, tiled...]
    all_to_all x3 -> x0, waiting for transfers between devices: 80.1 us -> none  [the longest x1 39.4 us: per_device(): lax.all_to_all(panel_geometry[asked], 'tiles', split_axis=0, concat_axis=...]
    pallas_call x0 -> x1, Pallas kernels: none -> 60.9 us  [per_device(): pl.pallas_call(functools.partial(kernel, slabs), out_shape=jax.ShapeDtype...]
    scatter-add x7 -> x0, other arithmetic: 38.8 us -> none  [the longest x1 24.6 us: per_device(): jnp.zeros((3, tile_count * vertex_width), jnp.float32).at[:, flat_ids]]
    all_to_all x1 -> x0, blocking collectives: 35.1 us -> none  [per_device(): lax.all_to_all(wanted, 'tiles', split_axis=0, concat_axis=0, tiled=True)]
    dot_general x28 -> x0, matrix products: 25.2 us -> none  [the longest x12 11.2 us: tile_terms(): jnp.einsum('apq,acq->acp', factor, points, precision=lax.Precision.HIGHEST)]
    all_to_all x3 -> x0, starting transfers between devices: 23.6 us -> none  [the longest x1 9.5 us: per_device(): lax.all_to_all(table, 'tiles', split_axis=0, concat_axis=0, tiled=True)]
    gather x13 -> x0, local copies, waits for them, and re-layouts: 14.1 us -> none  [the longest x4 5.06 us: accumulate(): adjoint_part[group_targets]]
  transfers between devices with their start and end apart: 4 -> 0, of which waited for: 4 -> 0; matrix products, arithmetic and copies ran while one was open for 1% -> 0% of each run, Pallas kernels for 0% -> 0%
where the time goes in v3:
time: 65.4 us; the launch traced here: 64.9 us
  Pallas kernels  60.9 us (93%)
  local copies, waits for them, and re-layouts  3.33 us (5%)
  between operations  0.72 us (1%)
    pallas_call x1, Pallas kernels, per_device(): pl.pallas_call(functools.partial(kernel, slabs), out_shape=jax.ShapeDtype...  60.9 us
    unnamed x17, local copies, waits for them, and re-layouts  3.33 us

profile of v3, /device:TPU:1, one launch (start us, length us, event | category | flops | bytes accessed | tf_op | source)
XLA Modules:
  0.0 64.9 jit_solution(7309745355282850310)
XLA Ops:
  0.0 0.0 copy-start
  0.7 0.0 copy-start.7
  0.7 0.0 copy-start.4
  0.7 0.0 copy-start.5
  0.7 0.0 copy-start.6
  0.7 0.0 copy-done
  0.7 0.6 copy-done.7
  1.3 0.0 copy-done.4
  1.3 0.0 copy-done.5
  1.4 0.0 copy-done.6
  1.4 0.0 copy-start.1
  1.4 0.7 %copy-done.1 = s32[4,4,128]{2,1,0:T(4,128)S(1)} copy-done((s32[4,4,128]{2,1,0:T(4,128)S(1)}, s32[4,4,128]{2,1,0:T(4,128)}, u32[]{:S(2)}) %copy-start.1) | copy-done | bytes 8216
  2.1 0.0 copy-start.2
  2.1 0.7 %copy-done.2 = bf16[4,4,128]{2,1,0:T(4,128)(2,1)S(1)} copy-done((bf16[4,4,128]{2,1,0:T(4,128)(2,1)S(1)}, bf16[4,4,128]{2,1,0:T(4,128)(2,1)}, u32[]{:S(2)}) %copy-start.2) | copy-done | bytes 4120
  2.8 0.0 copy-start.3
  2.8 0.7 %copy-done.3 = bf16[4,4,128]{2,1,0:T(4,128)(2,1)S(1)} copy-done((bf16[4,4,128]{2,1,0:T(4,128)(2,1)S(1)}, bf16[4,4,128]{2,1,0:T(4,128)(2,1)}, u32[]{:S(2)}) %copy-start.3) | copy-done | bytes 4120
  3.4 60.9 %gather_pairs_return.1 = f32[3,512]{1,0:T(4,128)S(1)} custom-call(f32[6,4,128]{2,1,0:T(4,128)S(1)} %bitcast.7, bf16[16,128]{1,0:T(8,128)(2,1)S(1)} %bitcast.8, bf16[16,128]{1,0:T(8,128)(2,1)S(1)} %bitcast.9, s32[1,32]{1,0:T(1,128)S(1)} %bitcast.10, s32[1,32]{1,0:T(1,128)S(1)} %bitcast.11, s32[1,32]{1,0:T(1,128)S(1)} %bitcast.12, s32[1,32]{1,0:T(1,128)S(1)} %bitcast.13, ...), custom_call_target="tpu_custom_call" | custom-call | tf_op jit(solution)/shard_map/gather_pairs_return/pallas_call | solution.py:461
  64.3 0.6 copy.12
Async XLA Ops:
  0.0 0.7 %copy-start = (f32[4,6,128]{2,0,1:T(4,128)S(1)}, f32[4,6,128]{2,0,1:T(4,128)}, u32[]{:S(2)}) copy-start(f32[4,6,128]{2,0,1:T(4,128)} %param.9) | copy-start | bytes 36868
  0.7 0.7 %copy-start.7 = (s32[32]{0:T(128)S(1)}, s32[32]{0:T(128)}, u32[]{:S(2)}) copy-start(s32[32]{0:T(128)} %param.15) | copy-start | bytes 388
  0.7 0.7 %copy-start.4 = (s32[32]{0:T(128)S(1)}, s32[32]{0:T(128)}, u32[]{:S(2)}) copy-start(s32[32]{0:T(128)} %param.12) | copy-start | bytes 388
  0.7 0.7 %copy-start.5 = (s32[32,1]{0,1:T(1,128)S(1)}, s32[32,1]{0,1:T(1,128)}, u32[]{:S(2)}) copy-start(s32[32,1]{0,1:T(1,128)} %param.13) | copy-start | bytes 388
  0.7 0.7 %copy-start.6 = (s32[32]{0:T(128)S(1)}, s32[32]{0:T(128)}, u32[]{:S(2)}) copy-start(s32[32]{0:T(128)} %param.14) | copy-start | bytes 388
  1.4 0.7 %copy-start.1 = (s32[4,4,128]{2,1,0:T(4,128)S(1)}, s32[4,4,128]{2,1,0:T(4,128)}, u32[]{:S(2)}) copy-start(s32[4,4,128]{2,1,0:T(4,128)} %corner_ref.1) | copy-start | bytes 24580
  2.1 0.7 %copy-start.2 = (bf16[4,4,128]{2,1,0:T(4,128)(2,1)S(1)}, bf16[4,4,128]{2,1,0:T(4,128)(2,1)}, u32[]{:S(2)}) copy-start(bf16[4,4,128]{2,1,0:T(4,128)(2,1)} %param.10) | copy-start | bytes 12292
  2.8 0.7 %copy-start.3 = (bf16[4,4,128]{2,1,0:T(4,128)(2,1)S(1)}, bf16[4,4,128]{2,1,0:T(4,128)(2,1)}, u32[]{:S(2)}) copy-start(bf16[4,4,128]{2,1,0:T(4,128)(2,1)} %param.11) | copy-start | bytes 12292

commit v4 on v3

--- a/solution.py
+++ b/solution.py
@@ -11,6 +11,7 @@
 FAR = 4
 PB = 128
 PAIRS_DEV = 32
+GROUP = 8
 MESH = pl.DeviceIdType.MESH
 F32 = jnp.float32
 BF16 = jnp.bfloat16
@@ -285,20 +286,33 @@
                 ).astype(BF16)
         source_acc[da] = jnp.zeros((4, 4, PB), F32)
 
-        def one_list(k, carry, da=da):
-            for occurrence in range(2):
-                code = codes[k, 2 * da + occurrence, 0]
-                order = code & 3
-                source = (code >> 2) & 3
-                target = (code >> 4) & 3
+        def some_lists(group, carry, da=da):
+            slots = []
+            for step in range(GROUP):
+                k = group * GROUP + step
+                for occurrence in range(2):
+                    code = codes[k, 2 * da + occurrence, 0]
+                    slots.append((k, code & 3, (code >> 2) & 3, (code >> 4) & 3))
+            products = []
+            for k, order, source, target in slots:
+                columns = left[k * 4 + target]
+                products.append(
+                    (
+                        jnp.dot(columns, right[source], preferred_element_type=F32),
+                        jnp.dot(
+                            columns,
+                            right_far[source * 2 + ((order + 1) >> 2)],
+                            preferred_element_type=F32,
+                        ),
+                    )
+                )
+            factors = []
+            for (k, order, source, target), (inner, sides) in zip(slots, products):
                 centre_weight = jnp.where(order == 1, 1.0, jnp.where(order == 3, 4.0 / 9.0, 0.0))
                 side_weight = jnp.where(order == 2, 0.5, jnp.where(order == 3, 5.0 / 18.0, 0.0))
                 shift_weight = jnp.where(
                     order == 2, 0.5 * ROOT_HALF, jnp.where(order == 3, 5.0 / 18.0 * ROOT_FIFTH, 0.0)
                 )
-                columns = left[k * 4 + target]
-                inner = jnp.dot(columns, right[source], preferred_element_type=F32)
-                sides = jnp.dot(columns, right_far[source * 2 + ((order + 1) >> 2)], preferred_element_type=F32)
                 roots = lax.rsqrt(inner[:, PB:])
                 pulls = lax.rsqrt(sides)
                 roots = roots * roots * roots
@@ -315,15 +329,22 @@
                     ],
                     axis=1,
                 )
-                rows = trow[k * 4 + target]
-                by_source = jnp.dot(rows, high, preferred_element_type=F32) + jnp.dot(
-                    rows, low, preferred_element_type=F32
-                )
-                lines = srow[source]
-                across = (((1,), (1,)), ((), ()))
-                by_target = lax.dot_general(
-                    lines, high, across, preferred_element_type=F32
-                ) + lax.dot_general(lines, low, across, preferred_element_type=F32)
+                factors.append((high, low))
+            sums = []
+            across = (((1,), (1,)), ((), ()))
+            for (k, order, source, target), (high, low) in zip(slots, factors):
+                rows, lines = trow[k * 4 + target], srow[source]
+                sums.append(
+                    (
+                        jnp.dot(rows, high, preferred_element_type=F32)
+                        + jnp.dot(rows, low, preferred_element_type=F32),
+                        lax.dot_general(lines, high, across, preferred_element_type=F32)
+                        + lax.dot_general(lines, low, across, preferred_element_type=F32),
+                    )
+                )
+            gathered = [source_acc[da, block] for block in range(4)]
+            returned = [None] * 4
+            for n, ((k, order, source, target), (by_source, by_target)) in enumerate(zip(slots, sums)):
                 points = sbase[source]
                 pulled = (
                     by_source[4:8, :PB]
@@ -339,11 +360,17 @@
                     - tinfo[k, target][0:4] * by_target[0:1]
                 )
                 for block in range(4):
-                    source_acc[da, block] += jnp.where(source == block, 1.0, 0.0) * pulled
-                    target_acc[k, block] += jnp.where(target == block, 1.0, 0.0) * pushed
+                    gathered[block] = gathered[block] + jnp.where(source == block, 1.0, 0.0) * pulled
+                    term = jnp.where(target == block, 1.0, 0.0) * pushed
+                    returned[block] = term if n % 2 == 0 else returned[block] + term
+                if n % 2:
+                    for block in range(4):
+                        target_acc[k, block] += returned[block]
+            for block in range(4):
+                source_acc[da, block] = gathered[block]
             return carry
 
-        lax.fori_loop(0, SLAB, one_list, 0)
+        lax.fori_loop(0, SLAB // GROUP, some_lists, 0)
 
         def send_source(da=da):
             send(
@@ -489,7 +516,7 @@
             pltpu.SemaphoreType.DMA((8,)),
         ],
         compiler_params=pltpu.CompilerParams(
-            collective_id=0, has_side_effects=True, vmem_limit_bytes=48 * 1024 * 1024
+            collective_id=0, has_side_effects=True
         ),
         name="gather_pairs_return",
     )(

time: 65.4 us -> 52.4 us (0.80)
  Pallas kernels: 60.9 us -> 50.2 us
  local copies, waits for them, and re-layouts: 3.33 us -> 1.3 us
    pallas_call x1, Pallas kernels: 60.9 us -> 50.2 us  [per_device(): pl.pallas_call(functools.partial(kernel, slabs), out_shape=jax.ShapeDtype...]
    unnamed x17 -> x1, local copies, waits for them, and re-layouts: 3.33 us -> 1.3 us
where the time goes in v4:
time: 52.4 us; the launch traced here: 52.2 us
  Pallas kernels  50.2 us (96%)
  local copies, waits for them, and re-layouts  1.3 us (2%)
  between operations  0.66 us (1%)
    pallas_call x1, Pallas kernels, per_device(): pl.pallas_call(functools.partial(kernel, slabs), out_shape=jax.ShapeDtype...  50.2 us
    unnamed x1, local copies, waits for them, and re-layouts  1.3 us

profile of v4, /device:TPU:1, one launch (start us, length us, event | category | flops | bytes accessed | tf_op | source)
XLA Modules:
  0.0 52.2 jit_solution(14778089794412534209)
XLA Ops:
  0.7 50.2 %gather_pairs_return.1 = f32[3,512]{1,0:T(4,128)} custom-call(f32[6,4,128]{2,1,0:T(4,128)} %bitcast.7, bf16[16,128]{1,0:T(8,128)(2,1)} %bitcast.8, bf16[16,128]{1,0:T(8,128)(2,1)} %bitcast.9, s32[1,32]{1,0:T(1,128)} %bitcast.10, s32[1,32]{1,0:T(1,128)} %bitcast.11, s32[1,32]{1,0:T(1,128)} %bitcast.12, s32[1,32]{1,0:T(1,128)} %bitcast.13, ...), custom_call_target="tpu_custom_call" | custom-call | tf_op jit(solution)/shard_map/gather_pairs_return/pallas_call | solution.py:488
  50.9 1.3 %copy.12 = f32[3,512]{1,0:T(4,128)} copy(f32[3,512]{1,0:T(4,128)} %gather_pairs_return.1) | data formatting | bytes 12288

commit v5 on v4

--- a/solution.py
+++ b/solution.py
@@ -55,6 +55,16 @@
 
 def kernel(
     slabs,
+    geom_in,
+    adj_in,
+    str_in,
+    tgt_in,
+    own_in,
+    src_in,
+    ord_in,
+    cnt_ref,
+    corner_in,
+    out_ref,
     geom_ref,
     adj_ref,
     str_ref,
@@ -62,9 +72,8 @@
     own_ref,
     src_ref,
     ord_ref,
-    cnt_ref,
     corner_ref,
-    out_ref,
+    load_sems,
     sgeom,
     sstr,
     tadj,
@@ -97,7 +106,26 @@
     other = jnp.logical_not(mine)
     barrier = pltpu.get_barrier_semaphore()
     near_first = {1: (0,), 2: (0, 1), 4: (0, 1, 3, 2)}[outer]
+    near_last = {1: (0,), 2: (1, 0), 4: (1, 3, 2, 0)}[outer]
     shifts = (0, 1, tiles - 1, tiles // 2)
+
+    loads = [
+        pltpu.make_async_copy(src, dst, load_sems.at[n])
+        for n, (src, dst) in enumerate(
+            (
+                (geom_in, geom_ref),
+                (tgt_in, tgt_ref),
+                (own_in, own_ref),
+                (src_in, src_ref),
+                (ord_in, ord_ref),
+                (str_in, str_ref),
+                (adj_in, adj_ref),
+                (corner_in, corner_ref),
+            )
+        )
+    ]
+    for load in loads:
+        load.start()
 
     def greet(device):
         pl.semaphore_signal(barrier, inc=1, device_id=device, device_id_type=MESH)
@@ -118,6 +146,9 @@
                 greet(((t + tiles - shifts[o]) % tiles, (y + dy) % FAR))
     for ds in range(1, SLAB):
         greet((z * SLAB + (s + ds) % SLAB, y))
+
+    for load in loads:
+        load.wait()
 
     lane = lax.broadcasted_iota(jnp.int32, (1, PB), 1)
     tinfo[s] = jnp.zeros((4, 8, PB), F32)
@@ -131,6 +162,10 @@
 
     pl.semaphore_wait(barrier, slabs - mine.astype(jnp.int32) + SLAB - 1 + 15)
 
+    for dy in range(1, FAR):
+        send(adj_ref, tadj.at[s, y], send_sems.at[2], recv_sems.at[2], (t, (y + dy) % FAR))
+    tadj[s, y] = adj_ref[...]
+
     def send_strengths(zt):
         da = (quarter - zt // FAR + outer) % outer
         send(str_ref, sstr.at[da, y], send_sems.at[0], str_sems.at[da], (zt * SLAB + s, home))
@@ -157,12 +192,9 @@
         sstr[0, y] = str_ref[...]
         sgeom[0] = geom_ref[...]
 
-    for dy in range(1, FAR):
-        send(adj_ref, tadj.at[s, y], send_sems.at[2], recv_sems.at[2], (t, (y + dy) % FAR))
     for ds in range(1, SLAB):
         peer = (z * SLAB + (s + ds) % SLAB, y)
         send(tinfo.at[s], tinfo.at[s], send_sems.at[3], recv_sems.at[3], peer)
-    tadj[s, y] = adj_ref[...]
     wait(tadj.at[s, pl.ds(0, FAR - 1)], recv_sems.at[2])
     for ds in range(1, SLAB):
         peer = (z * SLAB + (s + ds) % SLAB, y)
@@ -235,7 +267,7 @@
     lax.fori_loop(0, SLAB, prepare_list, 0)
     copy.wait()
 
-    for da in near_first:
+    for da in near_last:
         if da:
             wait(sstr.at[da], str_sems.at[da])
             wait(sgeom.at[da], geom_sems.at[da])
@@ -463,8 +495,16 @@
         wait(rs_source, send_sems.at[5])
 
 
+def resident(dims, dtype):
+    return pltpu.VMEM(dims, dtype)
+
+
 def vmem():
     return pl.BlockSpec(memory_space=pltpu.VMEM)
+
+
+def anywhere():
+    return pl.BlockSpec(memory_space=pl.ANY)
 
 
 def smem():
@@ -487,10 +527,19 @@
     row = lambda values: values.reshape(1, PAIRS_DEV)
     return pl.pallas_call(
         functools.partial(kernel, slabs),
-        out_shape=jax.ShapeDtypeStruct((3, WITHIN), F32),
-        in_specs=[vmem()] * 7 + [smem(), vmem()],
+        out_shape=resident((3, WITHIN), F32),
+        in_specs=[anywhere()] * 7 + [smem(), anywhere()],
         out_specs=vmem(),
         scratch_shapes=[
+            pltpu.VMEM((6, 4, PB), F32),
+            pltpu.VMEM((16, PB), BF16),
+            pltpu.VMEM((16, PB), BF16),
+            pltpu.VMEM((1, PAIRS_DEV), jnp.int32),
+            pltpu.VMEM((1, PAIRS_DEV), jnp.int32),
+            pltpu.VMEM((1, PAIRS_DEV), jnp.int32),
+            pltpu.VMEM((1, PAIRS_DEV), jnp.int32),
+            pltpu.VMEM((4, 4, PB), jnp.int32),
+            pltpu.SemaphoreType.DMA((8,)),
             pltpu.VMEM((outer, 6, 4, PB), F32),
             pltpu.VMEM((outer, FAR, 16, PB), BF16),
             pltpu.VMEM((SLAB, FAR, 16, PB), BF16),

time: 52.4 us -> 48.8 us (0.931)
  Pallas kernels: 50.2 us -> 47.4 us
  local copies, waits for them, and re-layouts: 1.3 us -> 0.6 us
    pallas_call x1, Pallas kernels: 50.2 us -> 47.4 us  [per_device(): pl.pallas_call(functools.partial(kernel, slabs), out_shape=resident((3, W...]
    unnamed x1, local copies, waits for them, and re-layouts: 1.3 us -> 0.6 us
where the time goes in v5:
time: 48.8 us; the launch traced here: 48.6 us
  Pallas kernels  47.4 us (97%)
  between operations  0.66 us (1%)
  local copies, waits for them, and re-layouts  0.6 us (1%)
    pallas_call x1, Pallas kernels, per_device(): pl.pallas_call(functools.partial(kernel, slabs), out_shape=resident((3, W...  47.4 us

profile of v5, /device:TPU:1, one launch (start us, length us, event | category | flops | bytes accessed | tf_op | source)
XLA Modules:
  0.0 48.6 jit_solution(6473958978409826232)
XLA Ops:
  0.7 47.4 %gather_pairs_return.1 = f32[3,512]{1,0:T(4,128)S(1)} custom-call(f32[6,4,128]{2,1,0:T(4,128)} %bitcast.7, bf16[16,128]{1,0:T(8,128)(2,1)} %bitcast.8, bf16[16,128]{1,0:T(8,128)(2,1)} %bitcast.9, s32[1,32]{1,0:T(1,128)} %bitcast.10, s32[1,32]{1,0:T(1,128)} %bitcast.11, s32[1,32]{1,0:T(1,128)} %bitcast.12, s32[1,32]{1,0:T(1,128)} %bitcast.13, ...), custom_call_target="tpu_custom_call" | custom-call | tf_op jit(solution)/shard_map/gather_pairs_return/pallas_call | solution.py:528
  48.0 0.6 %copy.11 = f32[3,512]{1,0:T(4,128)} copy(f32[3,512]{1,0:T(4,128)S(1)} %gather_pairs_return.1) | data formatting | bytes 12288

commit v6 on v5

--- a/solution.py
+++ b/solution.py
@@ -124,9 +124,6 @@
             )
         )
     ]
-    for load in loads:
-        load.start()
-
     def greet(device):
         pl.semaphore_signal(barrier, inc=1, device_id=device, device_id_type=MESH)
 
@@ -148,17 +145,20 @@
         greet((z * SLAB + (s + ds) % SLAB, y))
 
     for load in loads:
+        load.start()
+
+    for load in loads:
         load.wait()
 
     lane = lax.broadcasted_iota(jnp.int32, (1, PB), 1)
-    tinfo[s] = jnp.zeros((4, 8, PB), F32)
+    tinfo[s] = jnp.zeros((4, 4, PB), F32)
     for comp in range(3):
         for block in range(4):
             tinfo[s, block, comp : comp + 1, :] = geom_ref[comp, block : block + 1, :]
     live = lax.broadcasted_iota(jnp.int32, (1, PAIRS_DEV), 1) < cnt_ref[0]
     orders = jnp.where(live, ord_ref[...], 0)
     for row, values in enumerate((tgt_ref[...], own_ref[...], src_ref[...], orders)):
-        tinfo[s, 0, 4 + row : 5 + row, 0:PAIRS_DEV] = values.astype(F32)
+        tinfo[s, row, 3:4, 0:PAIRS_DEV] = values.astype(F32)
 
     pl.semaphore_wait(barrier, slabs - mine.astype(jnp.int32) + SLAB - 1 + 15)
 
@@ -227,8 +227,7 @@
         lax.broadcasted_iota(jnp.int32, (PB, PB), 0) < lax.broadcasted_iota(jnp.int32, (PB, PB), 1), 1.0, 0.0
     ).astype(BF16)
     for k in range(SLAB):
-        rows = tinfo[k, 0].astype(jnp.int32)
-        target, owner, source, order = (rows[r : r + 1] for r in range(4, 8))
+        target, owner, source, order = (tinfo[k, r, 3:4, :].astype(jnp.int32) for r in range(4))
         match = (owner == wanted) & (order > 0) & (wide_lane < PAIRS_DEV) & (da_of < outer)
         count = jnp.dot(
             jnp.where(match, 1.0, 0.0).astype(BF16), before, preferred_element_type=F32
@@ -245,10 +244,12 @@
     one = jnp.ones((1, PB), F32)
     zero1 = jnp.zeros((1, PB), F32)
 
+    tile_row = lax.broadcasted_iota(jnp.int32, (4, PB), 0)
+
     def prepare_list(k, carry):
         conditions = [tadj[k, yy].astype(F32) for yy in range(FAR)]
         for block in range(4):
-            centre = tinfo[k, block][0:4]
+            centre = jnp.where(tile_row < 3, tinfo[k, block], 0.0)
             high, middle, low = split(centre)
             sq = squares(centre, 0.0)
             stack = jnp.concatenate(
@@ -389,7 +390,7 @@
                     by_target[4:8]
                     + by_target[8:12]
                     + by_target[12:16]
-                    - tinfo[k, target][0:4] * by_target[0:1]
+                    - tinfo[k, target] * by_target[0:1]
                 )
                 for block in range(4):
                     gathered[block] = gathered[block] + jnp.where(source == block, 1.0, 0.0) * pulled
@@ -543,7 +544,7 @@
             pltpu.VMEM((outer, 6, 4, PB), F32),
             pltpu.VMEM((outer, FAR, 16, PB), BF16),
             pltpu.VMEM((SLAB, FAR, 16, PB), BF16),
-            pltpu.VMEM((SLAB, 4, 8, PB), F32),
+            pltpu.VMEM((SLAB, 4, 4, PB), F32),
             pltpu.VMEM((SLAB * 4, PB, 48), BF16),
             pltpu.VMEM((SLAB * 4, 16, PB), BF16),
             pltpu.VMEM((4, 8, PB), F32),

time: 48.8 us -> 48.8 us (level)
  no operation moved by 1% of the time
where the time goes in v6:
time: 48.8 us; the launch traced here: 48.6 us
  Pallas kernels  47.4 us (97%)
  between operations  0.66 us (1%)
  local copies, waits for them, and re-layouts  0.6 us (1%)
    pallas_call x1, Pallas kernels, per_device(): pl.pallas_call(functools.partial(kernel, slabs), out_shape=resident((3, W...  47.4 us

profile of v6, /device:TPU:1, one launch (start us, length us, event | category | flops | bytes accessed | tf_op | source)
XLA Modules:
  0.0 48.6 jit_solution(9356204955486766559)
XLA Ops:
  0.7 47.4 %gather_pairs_return.1 = f32[3,512]{1,0:T(4,128)S(1)} custom-call(f32[6,4,128]{2,1,0:T(4,128)} %bitcast.7, bf16[16,128]{1,0:T(8,128)(2,1)} %bitcast.8, bf16[16,128]{1,0:T(8,128)(2,1)} %bitcast.9, s32[1,32]{1,0:T(1,128)} %bitcast.10, s32[1,32]{1,0:T(1,128)} %bitcast.11, s32[1,32]{1,0:T(1,128)} %bitcast.12, s32[1,32]{1,0:T(1,128)} %bitcast.13, ...), custom_call_target="tpu_custom_call" | custom-call | tf_op jit(solution)/shard_map/gather_pairs_return/pallas_call | solution.py:529
  48.0 0.6 %copy.11 = f32[3,512]{1,0:T(4,128)} copy(f32[3,512]{1,0:T(4,128)S(1)} %gather_pairs_return.1) | data formatting | bytes 12288
